TPU v7x, 32 devices: a whole 2x2x4 slice. The times are simulated.
32 devices in a mesh: seq: 8 (over z, y), fsdp: 4 (over x, core).
Axes of the slice: x: 2, y: 2, z: 4, core: 2. Of those that a mesh axis runs over, the one named last changes fastest.
Arguments:
- activations: bfloat16 [4, 2048, 640], P('fsdp', 'seq')
- segments: int32 [4, 2048], P('fsdp', 'seq'), may hold values from 0 to 1, as said below
- positions: int32 [4, 2048], P('fsdp', 'seq'), may hold values from 0 to 1535, as said below
- cotangent: bfloat16 [4, 2048, 640], P('fsdp', 'seq'), may hold values from -6 to 6
- query_weight: bfloat16 [2, 640, 1024], P(None, 'fsdp'), may hold values from -0.25 to 0.25
- key_weight: bfloat16 [2, 640, 256], P(None, 'fsdp'), may hold values from -0.25 to 0.25
- value_weight: bfloat16 [2, 640, 256], P(None, 'fsdp'), may hold values from -0.25 to 0.25
- out_weight: bfloat16 [2, 1024, 640], P(None, 'fsdp'), may hold values from -0.375 to 0.375
- gate_weight: bfloat16 [2, 640, 2048], P(None, 'fsdp'), may hold values from -0.25 to 0.25
- up_weight: bfloat16 [2, 640, 2048], P(None, 'fsdp'), may hold values from -0.25 to 0.25
- down_weight: bfloat16 [2, 2048, 640], P(None, 'fsdp'), may hold values from -0.125 to 0.125
- norm_gains: bfloat16 [2, 4, 640], P(None, None, 'fsdp'), may hold values from 0.5 to 1.5
- head_gains: bfloat16 [2, 2, 256], P(None, None, 'fsdp'), may hold values from 0.5 to 1.5
Outputs:
- output: bfloat16 [4, 2048, 640], P('fsdp', 'seq')
- input_grad: bfloat16 [4, 2048, 640], P('fsdp', 'seq')
- query_grad: float32 [2, 640, 1024], P(None, 'fsdp')
- key_grad: float32 [2, 640, 256], P(None, 'fsdp')
- value_grad: float32 [2, 640, 256], P(None, 'fsdp')
- out_grad: float32 [2, 1024, 640], P(None, 'fsdp')
- gate_grad: float32 [2, 640, 2048], P(None, 'fsdp')
- up_grad: float32 [2, 640, 2048], P(None, 'fsdp')
- down_grad: float32 [2, 2048, 640], P(None, 'fsdp')
- norm_gain_grad: float32 [2, 4, 640], P(None, None, 'fsdp')
- head_gain_grad: float32 [2, 2, 256], P(None, None, 'fsdp')
Inputs may be any that keep to these rules, and one draw needn't show every extreme that they name: In each group, segments start at 0, never fall and rise by one at each sequence start; each sequence is contiguous. In the first group a sequence starts at token 1024. positions count tokens from 0 at the first token of each sequence.
All inputs are finite; a program needn't handle non-finite values.
Results may differ from a plain program's by a relative error of at most 0.024.
Values may be sent and summed in bfloat16 or wider, within the bound.
A program may use at most 256 MiB of HBM per device.

v0:
```python
import jax
import jax.numpy as jnp
from jax import lax
from jax.sharding import PartitionSpec as P

HEADS = 4
HD = 256
WINDOW = 512


EPS = 1e-06


def passed_along(value, axis, steps):
    count = lax.axis_size(axis)
    first, last = (max(0, -steps), min(count, count - steps))
    return lax.ppermute(value, axis, [(source, source + steps) for source in range(first, last)])


def rms_scale(values, gain_vec):
    return values * lax.rsqrt(jnp.mean(values * values, -1, keepdims=True) + EPS) * gain_vec


def rotate(values, cosine, sine_part):
    middle_at = values.shape[-1] // 2
    leading = values[..., :middle_at]
    trailing = values[..., middle_at:]
    return jnp.concatenate(
        [leading * cosine - trailing * sine_part, trailing * cosine + leading * sine_part], -1
    )


def angles(places):
    halfway = HD // 2
    frequency = 10000.0 ** (-(jnp.arange(halfway, dtype=jnp.float32) * 2.0 / HD))
    turned = places.astype(jnp.float32)[:, None] * frequency[None, :]
    return (jnp.cos(turned), jnp.sin(turned))


def gelu_gate(gate_vals, up_part):
    return jax.nn.gelu(gate_vals, approximate=True) * up_part


def outer_sum(first_op, second_op):
    return lax.dot_general(
        first_op, second_op, (((0,), (0,)), ((), ())), preferred_element_type=jnp.float32
    )


def back_dot(first_op, second_op):
    return lax.dot_general(
        first_op, second_op, (((1,), (1,)), ((), ())), preferred_element_type=jnp.float32
    )


def rim_sizes(tokens):
    reach = (WINDOW + tokens - 1) // tokens
    return [
        (shift_by, min(tokens, WINDOW - (shift_by - 1) * tokens))
        for shift_by in range(reach, 0, -1)
    ]


def block_scores(query_block, key_slab, seg_query, seg_key):
    scores = jnp.einsum(
        "qhd,kd->hqk", query_block, key_slab, preferred_element_type=jnp.float32
    ) * HD ** (-0.5)
    row_count = query_block.shape[0]
    span_keys = key_slab.shape[0]
    distance = (
        jnp.arange(row_count, dtype=jnp.int32)[:, None]
        - jnp.arange(span_keys, dtype=jnp.int32)[None, :]
        + WINDOW
    )
    allowed = (distance >= 0) & (distance < WINDOW) & (seg_query[:, None] == seg_key[None, :])
    return (scores, allowed[None])


def forward_layer(x, weights_now, seg_own, seg_ext, cosine, sine_part):
    query_mat, key_mat, value_mat, out_mat, gate_mat, up_mat, down_mat, model_gains, head_pair = (
        weights_now
    )
    tokens = x.shape[0]
    gains_now = model_gains.astype(jnp.float32)
    head_now = head_pair.astype(jnp.float32)
    normed, pull_in = jax.vjp(rms_scale, x, gains_now[0])
    hidden = normed.astype(jnp.bfloat16)
    query_raw = jnp.dot(hidden, query_mat, preferred_element_type=jnp.float32)
    key_raw = jnp.dot(hidden, key_mat, preferred_element_type=jnp.float32)
    values = jnp.dot(hidden, value_mat, preferred_element_type=jnp.float32).astype(jnp.bfloat16)

    def query_piece(raw_vals, gain_vec):
        return rotate(
            rms_scale(raw_vals.reshape(tokens, HEADS, HD), gain_vec),
            cosine[:, None, :],
            sine_part[:, None, :],
        )

    def key_piece(raw_vals, gain_vec):
        return rotate(rms_scale(raw_vals, gain_vec), cosine, sine_part)

    query_rot, pull_query = jax.vjp(query_piece, query_raw, head_now[0])
    key_rot, pull_key = jax.vjp(key_piece, key_raw, head_now[1])
    query_low = query_rot.astype(jnp.bfloat16)
    key_low = key_rot.astype(jnp.bfloat16)
    key_parts = []
    value_parts = []
    for shift_by, rim_rows in rim_sizes(tokens):
        got_key, got_value = passed_along((key_low, values), "seq", shift_by)
        key_parts.append(got_key)
        value_parts.append(got_value)
    key_ext = jnp.concatenate(key_parts + [key_low], 0)
    value_ext = jnp.concatenate(value_parts + [values], 0)
    scores, allowed = block_scores(query_low, key_ext, seg_own, seg_ext)
    masked = jnp.where(allowed, scores, -1e30)
    row_top = jnp.max(masked, -1, keepdims=True)
    raised = jnp.where(allowed, jnp.exp(masked - row_top), 0.0)
    row_total = jnp.sum(raised, -1, keepdims=True)
    attention = (raised / row_total).astype(jnp.bfloat16)
    outputs = jnp.einsum("hqk,kd->qhd", attention, value_ext, preferred_element_type=jnp.float32)
    row_tops = [row_top]
    totals = [row_total]
    attended = outputs.reshape(tokens, HEADS * HD).astype(jnp.bfloat16)
    projected = jnp.dot(attended, out_mat, preferred_element_type=jnp.float32)
    post_out, pull_post = jax.vjp(rms_scale, projected, gains_now[1])
    middle = x + post_out
    normed_two, pull_pre = jax.vjp(rms_scale, middle, gains_now[2])
    hidden_two = normed_two.astype(jnp.bfloat16)
    gate_vals = jnp.dot(hidden_two, gate_mat, preferred_element_type=jnp.float32)
    up_part = jnp.dot(hidden_two, up_mat, preferred_element_type=jnp.float32)
    activated, pull_act = jax.vjp(gelu_gate, gate_vals, up_part)
    act_low = activated.astype(jnp.bfloat16)
    ffn_out = jnp.dot(act_low, down_mat, preferred_element_type=jnp.float32)
    post_two, pull_ffn = jax.vjp(rms_scale, ffn_out, gains_now[3])
    retained = (
        hidden,
        query_low,
        key_ext,
        value_ext,
        row_tops,
        totals,
        attended,
        hidden_two,
        act_low,
        pull_in,
        pull_query,
        pull_key,
        pull_post,
        pull_pre,
        pull_act,
        pull_ffn,
    )
    return (middle + post_two, retained)


def backward_layer(upstream, weights_now, retained, seg_own, seg_ext):
    query_mat, key_mat, value_mat, out_mat, gate_mat, up_mat, down_mat, model_gains, head_pair = (
        weights_now
    )
    (
        hidden,
        query_low,
        key_ext,
        value_ext,
        row_tops,
        totals,
        attended,
        hidden_two,
        act_low,
        pull_in,
        pull_query,
        pull_key,
        pull_post,
        pull_pre,
        pull_act,
        pull_ffn,
    ) = retained
    tokens = upstream.shape[0]
    block_rows = min(512, tokens)
    grad_ffn, gain_ffn = pull_ffn(upstream)
    ffn_low = grad_ffn.astype(jnp.bfloat16)
    down_term = outer_sum(act_low, ffn_low)
    grad_act = back_dot(ffn_low, down_mat)
    grad_gate, grad_up = pull_act(grad_act)
    gate_low = grad_gate.astype(jnp.bfloat16)
    up_low = grad_up.astype(jnp.bfloat16)
    gate_term = outer_sum(hidden_two, gate_low)
    up_term = outer_sum(hidden_two, up_low)
    grad_hidden_two = back_dot(gate_low, gate_mat) + back_dot(up_low, up_mat)
    middle_part, gain_pre = pull_pre(grad_hidden_two)
    grad_middle = upstream + middle_part
    grad_proj, gain_post = pull_post(grad_middle)
    proj_low = grad_proj.astype(jnp.bfloat16)
    out_term = outer_sum(attended, proj_low)
    grad_att = back_dot(proj_low, out_mat).astype(jnp.bfloat16).reshape(tokens, HEADS, HD)
    key_back = jnp.zeros(key_ext.shape, jnp.float32)
    value_back = jnp.zeros(value_ext.shape, jnp.float32)
    query_parts = []
    for number, begin_at in enumerate(range(0, tokens, block_rows)):
        span_keys = block_rows + WINDOW
        scores, allowed = block_scores(query_low, key_ext, seg_own, seg_ext)
        masked = jnp.where(allowed, scores, -1e30)
        raised = jnp.where(allowed, jnp.exp(masked - row_tops[number]), 0.0)
        attention = raised / totals[number]
        attention_low = attention.astype(jnp.bfloat16)
        grad_prob = jnp.einsum(
            "qhd,kd->hqk", grad_att, value_ext, preferred_element_type=jnp.float32
        )
        spread = jnp.sum(grad_prob * attention, -1, keepdims=True)
        grad_scores = (attention * (grad_prob - spread)).astype(jnp.bfloat16)
        query_parts.append(
            jnp.einsum("hqk,kd->qhd", grad_scores, key_ext, preferred_element_type=jnp.float32)
            * HD ** (-0.5)
        )
        key_back = key_back.at[begin_at : begin_at + span_keys].add(
            jnp.einsum("hqk,qhd->kd", grad_scores, query_low, preferred_element_type=jnp.float32)
            * HD ** (-0.5)
        )
        value_back = value_back.at[begin_at : begin_at + span_keys].add(
            jnp.einsum("hqk,qhd->kd", attention_low, grad_att, preferred_element_type=jnp.float32)
        )
    key_own = key_back[WINDOW:]
    value_own = value_back[WINDOW:]
    offset = 0
    for shift_by, rim_rows in rim_sizes(tokens):
        got_key, got_value = (
            passed_along(
                key_back[offset : offset + rim_rows].astype(jnp.bfloat16), "seq", -shift_by
            ).astype(jnp.float32),
            passed_along(
                value_back[offset : offset + rim_rows].astype(jnp.bfloat16), "seq", -shift_by
            ).astype(jnp.float32),
        )
        key_own = key_own.at[tokens - rim_rows :].add(got_key)
        value_own = value_own.at[tokens - rim_rows :].add(got_value)
        offset = offset + rim_rows
    grad_query, gain_query = pull_query(query_parts[0])
    grad_key, gain_key = pull_key(key_own)
    query_grad_low = grad_query.astype(jnp.bfloat16)
    key_grad_low = grad_key.astype(jnp.bfloat16)
    value_grad_low = value_own.astype(jnp.bfloat16)
    query_term = outer_sum(hidden, query_grad_low)
    key_term = outer_sum(hidden, key_grad_low)
    value_term = outer_sum(hidden, value_grad_low)
    grad_hidden = (
        back_dot(query_grad_low, query_mat)
        + back_dot(key_grad_low, key_mat)
        + back_dot(value_grad_low, value_mat)
    )
    grad_input, gain_in = pull_in(grad_hidden)
    matrices = (query_term, key_term, value_term, out_term, gate_term, up_term, down_term)
    model_terms = jnp.stack([gain_in, gain_post, gain_pre, gain_ffn])
    head_terms = jnp.stack([gain_query, gain_key])
    return (grad_middle + grad_input, matrices, model_terms, head_terms)


def pack_terms(matrices, model_terms, head_terms, fsdp_size):
    columns = [matrix.reshape(fsdp_size, -1) for matrix in matrices]
    columns.append(model_terms.reshape(4, fsdp_size, -1).transpose(1, 0, 2).reshape(fsdp_size, -1))
    columns.append(head_terms.reshape(2, fsdp_size, -1).transpose(1, 0, 2).reshape(fsdp_size, -1))
    return jnp.concatenate(columns, 1)


def unpack_terms(summed, matrices, model_terms, head_terms, fsdp_size):
    shards = []
    offset = 0
    for matrix in matrices:
        length = matrix.size // fsdp_size
        shards.append(
            summed[offset : offset + length].reshape(matrix.shape[0] // fsdp_size, matrix.shape[1])
        )
        offset = offset + length
    length = model_terms.size // fsdp_size
    model_shard = summed[offset : offset + length].reshape(4, -1)
    offset = offset + length
    length = head_terms.size // fsdp_size
    head_shard = summed[offset : offset + length].reshape(2, -1)
    return (shards, model_shard, head_shard)


def local(
    activations,
    segments,
    positions,
    cotangent,
    query_weight,
    key_weight,
    value_weight,
    out_weight,
    gate_weight,
    up_weight,
    down_weight,
    norm_gains,
    head_gains,
):
    tokens = activations.shape[1]
    layers = query_weight.shape[0]
    fsdp_size = lax.axis_size("fsdp")
    seg_own = segments[0]
    seg_parts = []
    for shift_by, rim_rows in rim_sizes(tokens):
        seg_parts.append(passed_along(seg_own + 1, "seq", shift_by) - 1)
    seg_ext = jnp.concatenate(seg_parts + [seg_own], 0)
    cosine, sine_part = angles(positions[0])
    stream = activations[0].astype(jnp.float32)
    stored = []
    for layer_at in range(layers):
        weights_now = (
            lax.all_gather(query_weight[layer_at], "fsdp", axis=0, tiled=True),
            lax.all_gather(key_weight[layer_at], "fsdp", axis=0, tiled=True),
            lax.all_gather(value_weight[layer_at], "fsdp", axis=0, tiled=True),
            lax.all_gather(out_weight[layer_at], "fsdp", axis=0, tiled=True),
            lax.all_gather(gate_weight[layer_at], "fsdp", axis=0, tiled=True),
            lax.all_gather(up_weight[layer_at], "fsdp", axis=0, tiled=True),
            lax.all_gather(down_weight[layer_at], "fsdp", axis=0, tiled=True),
            lax.all_gather(norm_gains[layer_at], "fsdp", axis=1, tiled=True),
            lax.all_gather(head_gains[layer_at], "fsdp", axis=1, tiled=True),
        )
        stream, retained = forward_layer(stream, weights_now, seg_own, seg_ext, cosine, sine_part)
        stored.append((weights_now, retained))
    output = stream.astype(jnp.bfloat16)
    upstream = cotangent[0].astype(jnp.float32)
    collected = [None] * layers
    for layer_at in range(layers - 1, -1, -1):
        weights_now, retained = stored[layer_at]
        weights_now = (
            lax.all_gather(query_weight[layer_at], "fsdp", axis=0, tiled=True),
            lax.all_gather(key_weight[layer_at], "fsdp", axis=0, tiled=True),
            lax.all_gather(value_weight[layer_at], "fsdp", axis=0, tiled=True),
            lax.all_gather(out_weight[layer_at], "fsdp", axis=0, tiled=True),
            lax.all_gather(gate_weight[layer_at], "fsdp", axis=0, tiled=True),
            lax.all_gather(up_weight[layer_at], "fsdp", axis=0, tiled=True),
            lax.all_gather(down_weight[layer_at], "fsdp", axis=0, tiled=True),
            lax.all_gather(norm_gains[layer_at], "fsdp", axis=1, tiled=True),
            lax.all_gather(head_gains[layer_at], "fsdp", axis=1, tiled=True),
        )
        upstream, matrices, model_terms, head_terms = backward_layer(
            upstream, weights_now, retained, seg_own, seg_ext
        )
        packed = pack_terms(matrices, model_terms, head_terms, fsdp_size)
        groups = lax.axis_size("seq")
        own_part = lax.psum_scatter(
            packed.astype(jnp.bfloat16), "fsdp", scatter_dimension=0, tiled=True
        ).astype(jnp.float32)
        span_cols = own_part.shape[1] // groups
        piece = lax.psum_scatter(
            own_part.reshape(groups, span_cols), "seq", scatter_dimension=0, tiled=True
        )
        summed = (
            lax.all_gather(piece.astype(jnp.bfloat16), "seq", axis=0, tiled=True)
            .astype(piece.dtype)
            .reshape(-1)
        )
        collected[layer_at] = unpack_terms(summed, matrices, model_terms, head_terms, fsdp_size)
    input_grad = upstream.astype(jnp.bfloat16)
    stacked = [
        jnp.stack([collected[layer_at][0][number] for layer_at in range(layers)])
        for number in range(7)
    ]
    model_grad = jnp.stack([collected[layer_at][1] for layer_at in range(layers)])
    head_grad = jnp.stack([collected[layer_at][2] for layer_at in range(layers)])
    return (
        output[None],
        input_grad[None],
        stacked[0],
        stacked[1],
        stacked[2],
        stacked[3],
        stacked[4],
        stacked[5],
        stacked[6],
        model_grad,
        head_grad,
    )


def solution(mesh):
    placed = (
        P("fsdp", "seq", None),
        P("fsdp", "seq"),
        P("fsdp", "seq"),
        P("fsdp", "seq", None),
        P(None, "fsdp", None),
        P(None, "fsdp", None),
        P(None, "fsdp", None),
        P(None, "fsdp", None),
        P(None, "fsdp", None),
        P(None, "fsdp", None),
        P(None, "fsdp", None),
        P(None, None, "fsdp"),
        P(None, None, "fsdp"),
    )
    return jax.shard_map(
        local,
        mesh=mesh,
        in_specs=placed,
        out_specs=(
            P("fsdp", "seq", None),
            P("fsdp", "seq", None),
            P(None, "fsdp", None),
            P(None, "fsdp", None),
            P(None, "fsdp", None),
            P(None, "fsdp", None),
            P(None, "fsdp", None),
            P(None, "fsdp", None),
            P(None, "fsdp", None),
            P(None, None, "fsdp"),
            P(None, None, "fsdp"),
        ),
        check_vma=False,
    )
```

profile of v0, /device:TPU:0, one launch (start us, length us, event | category | flops | bytes accessed | tf_op | source)
XLA Modules:
  0.0 1682.6 jit_solution(11266598421061517749)
XLA Ops:
  18.7 9.1 all-gather
  28.1 6.6 all-gather.1
  34.9 9.0 slice_reduce_fusion.4
  51.5 5.4 all-gather.3
  57.2 6.4 all-gather.2
  79.6 6.0 all-gather.9
  86.0 9.5 slice_reduce_fusion
  95.5 8.8 all-gather.10
  104.4 6.4 all-gather.12
  114.2 6.7 all-gather.11
  140.5 5.2 multiply_convert_fusion.3
  153.7 4.3 collective-permute-start.6
  175.3 5.5 all-gather.45.cloned.1.call-done
  185.3 23.2 %all-gather.47.cloned.1.call-done = bf16[1,640,2048]{2,1,0:T(8,128)(2,1)} async-done(((bf16[1,160,2048]{2,1,0:T(8,128)(2,1)}), bf16[1,640,2048]{2,1,0:T(8,128)(2,1)}) %all-gather.47.cloned.1.call-update) | async-done | bytes 2621456 | tf_op jit(solution)/shard_map/all_gather | solution.py:313
  212.6 23.7 %all-gather.49.cloned.1.call-done = bf16[1,640,2048]{2,1,0:T(8,128)(2,1)} async-done(((bf16[1,160,2048]{2,1,0:T(8,128)(2,1)}), bf16[1,640,2048]{2,1,0:T(8,128)(2,1)}) %all-gather.49.cloned.1.call-update) | async-done | bytes 2621456 | tf_op jit(solution)/shard_map/all_gather | solution.py:314
  236.3 5.2 multiply_convert_fusion.2
  241.5 22.4 %all-gather.51.cloned.1.call-done = bf16[1,2048,640]{2,1,0:T(8,128)(2,1)} async-done(((bf16[1,512,640]{2,1,0:T(8,128)(2,1)}), bf16[1,2048,640]{2,1,0:T(8,128)(2,1)}) %all-gather.51.cloned.1.call-update) | async-done | bytes 2621456 | tf_op jit(solution)/shard_map/all_gather | solution.py:315
  314.3 5.4 reshape.887
  398.8 5.4 reshape.875
  437.1 385.9 %all-reduce.17.cloned.1.call-done = (bf16[4,1393408]{1,0:T(4,128)(2,1)}, bf16[4,1393408]{1,0:T(4,128)(2,1)}) async-done(((bf16[4,1393408]{1,0:T(4,128)(2,1)}, bf16[4,1393408]{1,0:T(4,128)(2,1)}), (bf16[4,1393408]{1,0:T(4,128)(2,1)}, bf16[4,1393408]{1,0:T(4,128)(2,1)})) %all-reduce.17.cloned.1.call-update) | async-done | bytes 22294544
  823.0 64.6 %fusion.2 = (f32[1393408]{0:T(1024)}, f32[1393408]{0:T(1024)}) fusion(bf16[4,1393408]{1,0:T(4,128)(2,1)} %get-tuple-element.289, u32[]{:T(128)} %bitcast.59, bf16[4,1393408]{1,0:T(4,128)(2,1)} %get-tuple-element.290), kind=kLoop, calls=%fused_computation.5 | loop fusion | flops 2786816 | bytes 16720900 | tf_op jit(solution)/shard_map/reshape | solution.py:347
  887.6 7.9 reshape.899
  895.5 8.0 reshape.897
  903.5 432.8 %all-reduce.18 = (bf16[8,174176]{1,0:T(8,128)(2,1)}, bf16[8,174176]{1,0:T(8,128)(2,1)S(1)}) all-reduce(f32[8,174176]{1,0:T(8,128)} %reshape.899, f32[8,174176]{1,0:T(8,128)} %reshape.897), channel_id=23, replica_groups=mesh['seq'=8,'fsdp'=4] {'seq'}, use_global_device_ids=true, to_apply=%region_45.46.clone | all-reduce | flops 2786816 | bytes 16720896
  1342.1 86.1 %all-gather.55.cloned.1.call-done = bf16[8,1,174176]{2,1,0:T(2,128)(2,1)} async-done(((bf16[1,1,174176]{2,1,0:T(2,128)(2,1)}), bf16[8,1,174176]{2,1,0:T(2,128)(2,1)}) %all-gather.55.cloned.1.call-update) | async-done | bytes 2786832 | tf_op jit(solution)/shard_map/all_gather | solution.py:350
  1428.2 60.2 %convert_reduce_fusion = f32[8,174176]{1,0:T(8,128)} fusion(bf16[8,1,174176]{2,1,0:T(2,128)(2,1)} %all-gather.55.cloned.1.call-done), kind=kLoop, calls=%fused_computation.2 | loop fusion | flops 1393408 | bytes 8360448 | tf_op jit(solution)/shard_map/convert_element_type | solution.py:351
  1488.4 8.2 reshape.893
  1500.5 18.9 %all-gather.53.cloned.1.call-done = bf16[8,1,174176]{2,1,0:T(2,128)(2,1)} async-done(((bf16[1,1,174176]{2,1,0:T(2,128)(2,1)}), bf16[8,1,174176]{2,1,0:T(2,128)(2,1)}) %all-gather.53.cloned.1.call-update) | async-done | bytes 2786832 | tf_op jit(solution)/shard_map/all_gather | solution.py:350
  1519.4 60.6 %convert_reduce_fusion.1 = f32[8,174176]{1,0:T(8,128)} fusion(bf16[8,1,174176]{2,1,0:T(2,128)(2,1)} %all-gather.53.cloned.1.call-done), kind=kLoop, calls=%fused_computation.3 | loop fusion | flops 1393408 | bytes 8360448 | tf_op jit(solution)/shard_map/convert_element_type | solution.py:351
  1580.0 8.1 reshape.881
  1598.2 20.9 %slice.472 = f32[10886,2,64]{2,1,0:T(2,128)} reshape(f32[8,174176]{1,0:T(8,128)} %convert_reduce_fusion) | data formatting | bytes 11147264 | tf_op jit(solution)/shard_map/slice | solution.py:277
  1619.1 20.8 %slice.470 = f32[10886,2,64]{2,1,0:T(2,128)} reshape(f32[8,174176]{1,0:T(8,128)} %convert_reduce_fusion.1) | data formatting | bytes 11147264 | tf_op jit(solution)/shard_map/slice | solution.py:277
  (712 shorter events, 308.4 us)
Async XLA Ops:
  7.2 117.1 %all-gather.33.cloned.1.call-start = ((), (), s32[]{:S(2)}) async-start(), calls=%async_computation | async-start | bytes 1638400 | tf_op jit(solution)/shard_map/all_gather | solution.py:309
  9.3 123.7 %all-gather.35.cloned.1.call-start = ((), (), s32[]{:S(2)}) async-start(), calls=%async_computation.1 | async-start | bytes 1638400 | tf_op jit(solution)/shard_map/all_gather | solution.py:312
  11.4 124.8 %all-gather.37.cloned.1.call-start = ((), (), s32[]{:S(2)}) async-start(), calls=%async_computation.2 | async-start | bytes 3276800 | tf_op jit(solution)/shard_map/all_gather | solution.py:313
  12.7 127.8 %all-gather.39.cloned.1.call-start = ((), (), s32[]{:S(2)}) async-start(), calls=%async_computation.3 | async-start | bytes 3276800 | tf_op jit(solution)/shard_map/all_gather | solution.py:314
  13.9 131.8 %all-gather.41.cloned.1.call-start = ((), (), s32[]{:S(2)}) async-start(), calls=%async_computation.4 | async-start | bytes 3276800 | tf_op jit(solution)/shard_map/all_gather | solution.py:315
  15.6 149.8 %all-gather.43.cloned.1.call-start = ((), (), s32[]{:S(2)}) async-start(), calls=%async_computation.5 | async-start | bytes 1638400 | tf_op jit(solution)/shard_map/all_gather | solution.py:309
  16.2 164.7 %all-gather.45.cloned.1.call-start = ((), (), s32[]{:S(2)}) async-start(), calls=%async_computation.6 | async-start | bytes 1638400 | tf_op jit(solution)/shard_map/all_gather | solution.py:312
  16.9 191.6 %all-gather.47.cloned.1.call-start = ((), (), s32[]{:S(2)}) async-start(), calls=%async_computation.7 | async-start | bytes 3276800 | tf_op jit(solution)/shard_map/all_gather | solution.py:313
  17.7 218.6 %all-gather.49.cloned.1.call-start = ((), (), s32[]{:S(2)}) async-start(), calls=%async_computation.8 | async-start | bytes 3276800 | tf_op jit(solution)/shard_map/all_gather | solution.py:314
  18.4 245.4 %all-gather.51.cloned.1.call-start = ((), (), s32[]{:S(2)}) async-start(), calls=%async_computation.9 | async-start | bytes 3276800 | tf_op jit(solution)/shard_map/all_gather | solution.py:315
  44.3 86.4 %collective-permute-start.1 = (bf16[256,256]{1,0:T(8,128)(2,1)S(1)}, bf16[256,256]{1,0:T(8,128)(2,1)S(1)}, u32[]{:S(2)}, u32[]{:S(2)}) collective-permute-start(bf16[256,256]{1,0:T(8,128)(2,1)S(1)} %convolution_convert_fusion.17), channel_id=1, source_target_pairs={{0,4},{4,8},{8,12},{12,16},{16,20},{20,24},{24,28},{1,5},{5,9},{9,... | collective-permute-start | bytes 393224 | tf_op jit(solution)/shard_map/ppermute | solution.py:17
  47.8 82.9 %collective-permute-start = (bf16[256,256]{1,0:T(8,128)(2,1)S(1)}, bf16[256,256]{1,0:T(8,128)(2,1)S(1)}, u32[]{:S(2)}, u32[]{:S(2)}) collective-permute-start(bf16[256,256]{1,0:T(8,128)(2,1)S(1)} %convolution_convert_fusion.17), channel_id=1, source_target_pairs={{0,8},{4,12},{8,16},{12,20},{16,24},{20,28},{1,9},{5,13},{9,17},{1... | collective-permute-start | bytes 393224 | tf_op jit(solution)/shard_map/ppermute | solution.py:17
  68.9 59.3 %collective-permute-start.5 = (bf16[256,256]{0,1:T(8,128)(2,1)S(1)}, bf16[256,256]{0,1:T(8,128)(2,1)S(1)}, u32[]{:S(2)}, u32[]{:S(2)}) collective-permute-start(bf16[256,256]{0,1:T(8,128)(2,1)S(1)} %pad_maximum_fusion.13), channel_id=1, source_target_pairs={{0,4},{4,8},{8,12},{12,16},{16,20},{20,24},{24,28},{1,5},{5,9},{9,... | collective-permute-start | bytes 393224 | tf_op jit(solution)/shard_map/ppermute | solution.py:17
  72.4 55.8 %collective-permute-start.4 = (bf16[256,256]{0,1:T(8,128)(2,1)S(1)}, bf16[256,256]{0,1:T(8,128)(2,1)S(1)}, u32[]{:S(2)}, u32[]{:S(2)}) collective-permute-start(bf16[256,256]{0,1:T(8,128)(2,1)S(1)} %pad_maximum_fusion.13), channel_id=1, source_target_pairs={{0,8},{4,12},{8,16},{12,20},{16,24},{20,28},{1,9},{5,13},{9,17},{1... | collective-permute-start | bytes 393224 | tf_op jit(solution)/shard_map/ppermute | solution.py:17
  75.9 44.9 %collective-permute-start.3 = (s32[256]{0:T(256)S(1)}, s32[256]{0:T(256)S(1)}, u32[]{:S(2)}, u32[]{:S(2)}) collective-permute-start(s32[256]{0:T(256)S(1)} %broadcast_add_fusion.2), channel_id=1, source_target_pairs={{0,4},{4,8},{8,12},{12,16},{16,20},{20,24},{24,28},{1,5},{5,9},{9,... | collective-permute-start | bytes 3080 | tf_op jit(solution)/shard_map/ppermute | solution.py:17
  79.4 743.6 %all-reduce.17.cloned.1.call-start = ((), (), s32[]{:S(2)}) async-start(), calls=%async_computation.12 | async-start | bytes 44589056
  120.9 3.2 collective-permute-start.2
  150.0 149.4 %copy-start.5 = (bf16[256,640]{1,0:T(8,128)(2,1)}, bf16[256,640]{1,0:T(8,128)(2,1)S(1)}, u32[]{:S(2)}) copy-start(bf16[256,640]{1,0:T(8,128)(2,1)S(1)} %multiply_convert_fusion.5) | copy-start | bytes 983044
  151.0 21.0 %collective-permute-start.7 = (bf16[256,256]{1,0:T(8,128)(2,1)}, bf16[256,256]{1,0:T(8,128)(2,1)}, u32[]{:S(2)}, u32[]{:S(2)}) collective-permute-start(bf16[256,256]{1,0:T(8,128)(2,1)} %convolution_convert_fusion.16), channel_id=1, source_target_pairs={{0,4},{4,8},{8,12},{12,16},{16,20},{20,24},{24,28},{1,5},{5,9},{9,... | collective-permute-start | bytes 393224 | tf_op jit(solution)/shard_map/ppermute | solution.py:17
  153.7 18.3 %collective-permute-start.6 = (bf16[256,256]{1,0:T(8,128)(2,1)}, bf16[256,256]{1,0:T(8,128)(2,1)}, u32[]{:S(2)}, u32[]{:S(2)}) collective-permute-start(bf16[256,256]{1,0:T(8,128)(2,1)} %convolution_convert_fusion.16), channel_id=1, source_target_pairs={{0,8},{4,12},{8,16},{12,20},{16,24},{20,28},{1,9},{5,13},{9,17},{1... | collective-permute-start | bytes 393224 | tf_op jit(solution)/shard_map/ppermute | solution.py:17
  159.8 8.7 collective-permute-start.9
  163.1 5.4 collective-permute-start.8
  292.0 35.6 %collective-permute-start.11 = (bf16[256,256]{0,1:T(8,128)(2,1)}, bf16[256,256]{0,1:T(8,128)(2,1)}, u32[]{:S(2)}, u32[]{:S(2)}) collective-permute-start(bf16[256,256]{0,1:T(8,128)(2,1)} %get-tuple-element.345), channel_id=1, source_target_pairs={{4,0},{8,4},{12,8},{16,12},{20,16},{24,20},{28,24},{5,1},{9,5},{13... | collective-permute-start | bytes 393224 | tf_op jit(solution)/shard_map/ppermute | solution.py:17
  293.3 34.3 %collective-permute-start.10 = (bf16[256,256]{0,1:T(8,128)(2,1)}, bf16[256,256]{0,1:T(8,128)(2,1)}, u32[]{:S(2)}, u32[]{:S(2)}) collective-permute-start(bf16[256,256]{0,1:T(8,128)(2,1)} %get-tuple-element.344), channel_id=1, source_target_pairs={{8,0},{12,4},{16,8},{20,12},{24,16},{28,20},{9,1},{13,5},{17,9},{2... | collective-permute-start | bytes 393224 | tf_op jit(solution)/shard_map/ppermute | solution.py:17
  298.2 36.1 %collective-permute-start.13 = (bf16[256,256]{1,0:T(8,128)(2,1)}, bf16[256,256]{1,0:T(8,128)(2,1)}, u32[]{:S(2)}, u32[]{:S(2)}) collective-permute-start(bf16[256,256]{1,0:T(8,128)(2,1)} %get-tuple-element.343), channel_id=1, source_target_pairs={{4,0},{8,4},{12,8},{16,12},{20,16},{24,20},{28,24},{5,1},{9,5},{13... | collective-permute-start | bytes 393224 | tf_op jit(solution)/shard_map/ppermute | solution.py:17
  306.5 27.9 %collective-permute-start.12 = (bf16[256,256]{1,0:T(8,128)(2,1)}, bf16[256,256]{1,0:T(8,128)(2,1)}, u32[]{:S(2)}, u32[]{:S(2)}) collective-permute-start(bf16[256,256]{1,0:T(8,128)(2,1)} %get-tuple-element.342), channel_id=1, source_target_pairs={{8,0},{12,4},{16,8},{20,12},{24,16},{28,20},{9,1},{13,5},{17,9},{2... | collective-permute-start | bytes 393224 | tf_op jit(solution)/shard_map/ppermute | solution.py:17
  359.6 48.0 %collective-permute-start.15 = (bf16[256,256]{0,1:T(8,128)(2,1)}, bf16[256,256]{0,1:T(8,128)(2,1)}, u32[]{:S(2)}, u32[]{:S(2)}) collective-permute-start(bf16[256,256]{0,1:T(8,128)(2,1)} %get-tuple-element.341), channel_id=1, source_target_pairs={{4,0},{8,4},{12,8},{16,12},{20,16},{24,20},{28,24},{5,1},{9,5},{13... | collective-permute-start | bytes 393224 | tf_op jit(solution)/shard_map/ppermute | solution.py:17
  361.0 46.7 %collective-permute-start.14 = (bf16[256,256]{0,1:T(8,128)(2,1)}, bf16[256,256]{0,1:T(8,128)(2,1)}, u32[]{:S(2)}, u32[]{:S(2)}) collective-permute-start(bf16[256,256]{0,1:T(8,128)(2,1)} %get-tuple-element.340), channel_id=1, source_target_pairs={{8,0},{12,4},{16,8},{20,12},{24,16},{28,20},{9,1},{13,5},{17,9},{2... | collective-permute-start | bytes 393224 | tf_op jit(solution)/shard_map/ppermute | solution.py:17
  364.7 48.3 %collective-permute-start.17 = (bf16[256,256]{1,0:T(8,128)(2,1)}, bf16[256,256]{1,0:T(8,128)(2,1)}, u32[]{:S(2)}, u32[]{:S(2)}) collective-permute-start(bf16[256,256]{1,0:T(8,128)(2,1)} %get-tuple-element.339), channel_id=1, source_target_pairs={{4,0},{8,4},{12,8},{16,12},{20,16},{24,20},{28,24},{5,1},{9,5},{13... | collective-permute-start | bytes 393224 | tf_op jit(solution)/shard_map/ppermute | solution.py:17
  366.0 47.0 %collective-permute-start.16 = (bf16[256,256]{1,0:T(8,128)(2,1)}, bf16[256,256]{1,0:T(8,128)(2,1)}, u32[]{:S(2)}, u32[]{:S(2)}) collective-permute-start(bf16[256,256]{1,0:T(8,128)(2,1)} %get-tuple-element.338), channel_id=1, source_target_pairs={{8,0},{12,4},{16,8},{20,12},{24,16},{28,20},{9,1},{13,5},{17,9},{2... | collective-permute-start | bytes 393224 | tf_op jit(solution)/shard_map/ppermute | solution.py:17
  434.3 993.9 %all-gather.55.cloned.1.call-start = ((), (), s32[]{:S(2)}) async-start(), calls=%async_computation.11 | async-start | bytes 6271488 | tf_op jit(solution)/shard_map/all_gather | solution.py:350
  1339.8 179.6 %all-gather.53.cloned.1.call-start = ((), (), s32[]{:S(2)}) async-start(), calls=%async_computation.10 | async-start | bytes 6271488 | tf_op jit(solution)/shard_map/all_gather | solution.py:350
  (200 other events, 1868.7 us)
Sparse Core Ops, SparseCore 0:
  10.2 22.6 all-gather.32
  35.0 18.1 all-gather.34
  55.3 26.0 all-gather.36
  83.4 29.7 all-gather.38
  114.6 25.5 all-gather.40
  142.2 18.1 all-gather.42
  162.6 18.1 all-gather.44
  183.0 25.5 all-gather.46
  210.7 25.5 all-gather.48
  238.3 25.5 all-gather.50
  434.4 388.4 all-reduce.16
  1340.0 88.1 all-gather.54
  1430.9 88.4 all-gather.52
where the time goes:
time: 1690 us; the launch traced here: 1680 us
  waiting for transfers between devices  570 us (34%)
  blocking collectives  488 us (29%)
  local copies, waits for them, and re-layouts  251 us (15%)
  other arithmetic  226 us (13%)
  matrix products  87.6 us (5%)
  starting transfers between devices  43.5 us (3%)
  between operations  16.9 us (1%)
    unnamed x1, blocking collectives  433 us
    unnamed x14, waiting for transfers between devices  389 us
    convert_element_type x2, other arithmetic, local(): summed = lax.all_gather(piece.astype(jnp.bfloat16), 'seq', axis=0, tiled=...  121 us
    all_gather x2, waiting for transfers between devices, local(): lax.all_gather(piece.astype(jnp.bfloat16), 'seq', axis=0, tiled=True)  105 us
    reshape x1, other arithmetic, local(): own_part.reshape(groups, span_cols)  64.6 us
    unnamed x418, local copies, waits for them, and re-layouts  53.9 us
    ppermute x18, starting transfers between devices, passed_along(): lax.ppermute(value, axis, [(source, source + steps) for source in range(f...  42.6 us
    slice x6, local copies, waits for them, and re-layouts, unpack_terms(): head_shard = summed[offset:offset + length].reshape(2, -1)  41.8 us
  transfers between devices with their start and end apart: 31, of which 8 were waited for; matrix products, arithmetic and copies ran while one was open for 14% of the time, Pallas kernels for 0%

commit v1 on v0

--- a/solution.py
+++ b/solution.py
@@ -15,6 +15,61 @@
     count = lax.axis_size(axis)
     first, last = (max(0, -steps), min(count, count - steps))
     return lax.ppermute(value, axis, [(source, source + steps) for source in range(first, last)])
+
+
+def swapped(value, axis, bit):
+    count = lax.axis_size(axis)
+    return lax.ppermute(value, axis, [(source, source ^ bit) for source in range(count)])
+
+
+def axis_bits(axis):
+    bits = []
+    bit = 1
+    while bit < lax.axis_size(axis):
+        bits.append(bit)
+        bit = 2 * bit
+    return bits
+
+
+def chosen(value, at, dim):
+    return lax.dynamic_index_in_dim(value, at, dim, keepdims=False)
+
+
+def added(first_op, second_op):
+    return (first_op.astype(jnp.float32) + second_op.astype(jnp.float32)).astype(jnp.bfloat16)
+
+
+def summed_shard(term):
+    shards = lax.axis_size("fsdp")
+    index = lax.axis_index("fsdp")
+    part = term.reshape(shards, term.shape[0] // shards, term.shape[1])
+    for bit in axis_bits("fsdp"):
+        mine = (index // bit) % 2
+        pairs = part.reshape(part.shape[0] // 2, 2, part.shape[1], part.shape[2])
+        got = swapped(chosen(pairs, 1 - mine, 1), "fsdp", bit)
+        part = added(chosen(pairs, mine, 1), got)
+    part = part[0]
+    blocks = lax.axis_size("seq")
+    index = lax.axis_index("seq")
+    dim = 0 if part.shape[0] % (16 * blocks) == 0 else 1
+    for bit in axis_bits("seq"):
+        mine = (index // bit) % 2
+        half = part.shape[dim] // 2
+        away = lax.dynamic_slice_in_dim(part, (1 - mine) * half, half, dim)
+        got = swapped(away, "seq", bit)
+        part = added(lax.dynamic_slice_in_dim(part, mine * half, half, dim), got)
+    for bit in axis_bits("seq")[::-1]:
+        first = (index // bit) % 2 == 0
+        got = swapped(part, "seq", bit)
+        part = jnp.concatenate([jnp.where(first, part, got), jnp.where(first, got, part)], dim)
+    return part.astype(jnp.float32)
+
+
+def summed_everywhere(values):
+    for axis in ("fsdp", "seq"):
+        for bit in axis_bits(axis):
+            values = values + swapped(values, axis, bit)
+    return values
 
 
 def rms_scale(values, gain_vec):
@@ -77,17 +132,16 @@
 
 
 def forward_layer(x, weights_now, seg_own, seg_ext, cosine, sine_part):
-    query_mat, key_mat, value_mat, out_mat, gate_mat, up_mat, down_mat, model_gains, head_pair = (
-        weights_now
-    )
+    qkv_mat, out_mat, both_mat, down_mat, model_gains, head_pair = weights_now
     tokens = x.shape[0]
     gains_now = model_gains.astype(jnp.float32)
     head_now = head_pair.astype(jnp.float32)
     normed, pull_in = jax.vjp(rms_scale, x, gains_now[0])
     hidden = normed.astype(jnp.bfloat16)
-    query_raw = jnp.dot(hidden, query_mat, preferred_element_type=jnp.float32)
-    key_raw = jnp.dot(hidden, key_mat, preferred_element_type=jnp.float32)
-    values = jnp.dot(hidden, value_mat, preferred_element_type=jnp.float32).astype(jnp.bfloat16)
+    raw_all = jnp.dot(hidden, qkv_mat, preferred_element_type=jnp.float32)
+    query_raw = raw_all[:, : HEADS * HD]
+    key_raw = raw_all[:, HEADS * HD : HEADS * HD + HD]
+    values = raw_all[:, HEADS * HD + HD :].astype(jnp.bfloat16)
 
     def query_piece(raw_vals, gain_vec):
         return rotate(
@@ -126,8 +180,9 @@
     middle = x + post_out
     normed_two, pull_pre = jax.vjp(rms_scale, middle, gains_now[2])
     hidden_two = normed_two.astype(jnp.bfloat16)
-    gate_vals = jnp.dot(hidden_two, gate_mat, preferred_element_type=jnp.float32)
-    up_part = jnp.dot(hidden_two, up_mat, preferred_element_type=jnp.float32)
+    both_vals = jnp.dot(hidden_two, both_mat, preferred_element_type=jnp.float32)
+    gate_vals = both_vals[:, : both_vals.shape[1] // 2]
+    up_part = both_vals[:, both_vals.shape[1] // 2 :]
     activated, pull_act = jax.vjp(gelu_gate, gate_vals, up_part)
     act_low = activated.astype(jnp.bfloat16)
     ffn_out = jnp.dot(act_low, down_mat, preferred_element_type=jnp.float32)
@@ -154,9 +209,7 @@
 
 
 def backward_layer(upstream, weights_now, retained, seg_own, seg_ext):
-    query_mat, key_mat, value_mat, out_mat, gate_mat, up_mat, down_mat, model_gains, head_pair = (
-        weights_now
-    )
+    qkv_mat, out_mat, both_mat, down_mat, model_gains, head_pair = weights_now
     (
         hidden,
         query_low,
@@ -179,19 +232,17 @@
     block_rows = min(512, tokens)
     grad_ffn, gain_ffn = pull_ffn(upstream)
     ffn_low = grad_ffn.astype(jnp.bfloat16)
-    down_term = outer_sum(act_low, ffn_low)
+    down_grad = summed_shard(outer_sum(act_low, ffn_low).astype(jnp.bfloat16))
     grad_act = back_dot(ffn_low, down_mat)
     grad_gate, grad_up = pull_act(grad_act)
-    gate_low = grad_gate.astype(jnp.bfloat16)
-    up_low = grad_up.astype(jnp.bfloat16)
-    gate_term = outer_sum(hidden_two, gate_low)
-    up_term = outer_sum(hidden_two, up_low)
-    grad_hidden_two = back_dot(gate_low, gate_mat) + back_dot(up_low, up_mat)
+    both_low = jnp.concatenate([grad_gate, grad_up], 1).astype(jnp.bfloat16)
+    both_grad = summed_shard(outer_sum(hidden_two, both_low).astype(jnp.bfloat16))
+    grad_hidden_two = back_dot(both_low, both_mat)
     middle_part, gain_pre = pull_pre(grad_hidden_two)
     grad_middle = upstream + middle_part
     grad_proj, gain_post = pull_post(grad_middle)
     proj_low = grad_proj.astype(jnp.bfloat16)
-    out_term = outer_sum(attended, proj_low)
+    out_grad = summed_shard(outer_sum(attended, proj_low).astype(jnp.bfloat16))
     grad_att = back_dot(proj_low, out_mat).astype(jnp.bfloat16).reshape(tokens, HEADS, HD)
     key_back = jnp.zeros(key_ext.shape, jnp.float32)
     value_back = jnp.zeros(value_ext.shape, jnp.float32)
@@ -236,46 +287,30 @@
         offset = offset + rim_rows
     grad_query, gain_query = pull_query(query_parts[0])
     grad_key, gain_key = pull_key(key_own)
-    query_grad_low = grad_query.astype(jnp.bfloat16)
-    key_grad_low = grad_key.astype(jnp.bfloat16)
-    value_grad_low = value_own.astype(jnp.bfloat16)
-    query_term = outer_sum(hidden, query_grad_low)
-    key_term = outer_sum(hidden, key_grad_low)
-    value_term = outer_sum(hidden, value_grad_low)
-    grad_hidden = (
-        back_dot(query_grad_low, query_mat)
-        + back_dot(key_grad_low, key_mat)
-        + back_dot(value_grad_low, value_mat)
-    )
+    qkv_low = jnp.concatenate(
+        [
+            grad_query.astype(jnp.bfloat16),
+            grad_key.astype(jnp.bfloat16),
+            value_own.astype(jnp.bfloat16),
+        ],
+        1,
+    )
+    qkv_grad = summed_shard(outer_sum(hidden, qkv_low).astype(jnp.bfloat16))
+    grad_hidden = back_dot(qkv_low, qkv_mat)
     grad_input, gain_in = pull_in(grad_hidden)
-    matrices = (query_term, key_term, value_term, out_term, gate_term, up_term, down_term)
-    model_terms = jnp.stack([gain_in, gain_post, gain_pre, gain_ffn])
-    head_terms = jnp.stack([gain_query, gain_key])
-    return (grad_middle + grad_input, matrices, model_terms, head_terms)
-
-
-def pack_terms(matrices, model_terms, head_terms, fsdp_size):
-    columns = [matrix.reshape(fsdp_size, -1) for matrix in matrices]
-    columns.append(model_terms.reshape(4, fsdp_size, -1).transpose(1, 0, 2).reshape(fsdp_size, -1))
-    columns.append(head_terms.reshape(2, fsdp_size, -1).transpose(1, 0, 2).reshape(fsdp_size, -1))
-    return jnp.concatenate(columns, 1)
-
-
-def unpack_terms(summed, matrices, model_terms, head_terms, fsdp_size):
-    shards = []
-    offset = 0
-    for matrix in matrices:
-        length = matrix.size // fsdp_size
-        shards.append(
-            summed[offset : offset + length].reshape(matrix.shape[0] // fsdp_size, matrix.shape[1])
-        )
-        offset = offset + length
-    length = model_terms.size // fsdp_size
-    model_shard = summed[offset : offset + length].reshape(4, -1)
-    offset = offset + length
-    length = head_terms.size // fsdp_size
-    head_shard = summed[offset : offset + length].reshape(2, -1)
-    return (shards, model_shard, head_shard)
+    gain_terms = jnp.concatenate([gain_in, gain_post, gain_pre, gain_ffn, gain_query, gain_key])
+    query_cols = HEADS * HD
+    ffn_cols = both_grad.shape[1] // 2
+    shards = (
+        qkv_grad[:, :query_cols],
+        qkv_grad[:, query_cols : query_cols + HD],
+        qkv_grad[:, query_cols + HD :],
+        out_grad,
+        both_grad[:, :ffn_cols],
+        both_grad[:, ffn_cols:],
+        down_grad,
+    )
+    return (grad_middle + grad_input, shards, summed_everywhere(gain_terms))
 
 
 def local(
@@ -303,55 +338,58 @@
     seg_ext = jnp.concatenate(seg_parts + [seg_own], 0)
     cosine, sine_part = angles(positions[0])
     stream = activations[0].astype(jnp.float32)
+    width = norm_gains.shape[2]
+    head_width = head_gains.shape[2]
+    gain_cols = jnp.concatenate(
+        [
+            norm_gains.reshape(layers * 4, width).T,
+            jnp.pad(head_gains.reshape(layers * 2, head_width).T, ((0, width - head_width), (0, 0))),
+        ],
+        1,
+    )
+
+    def gathered(part):
+        return lax.all_gather(part, "fsdp", axis=0, tiled=True)
+
     stored = []
     for layer_at in range(layers):
+        qkv_parts = [query_weight[layer_at], key_weight[layer_at], value_weight[layer_at]]
+        if layer_at == 0:
+            qkv_parts.append(gain_cols)
+        qkv_mat = gathered(jnp.concatenate(qkv_parts, 1))
+        if layer_at == 0:
+            gains_all = qkv_mat[:, (HEADS + 2) * HD :].astype(jnp.float32)
+            model_all = gains_all[:, : layers * 4].T.reshape(layers, 4, -1)
+            head_all = gains_all.reshape(fsdp_size, width, -1)[:, :head_width, layers * 4 :]
+            head_all = head_all.reshape(HD, layers * 2).T.reshape(layers, 2, HD)
+            qkv_mat = qkv_mat[:, : (HEADS + 2) * HD]
         weights_now = (
-            lax.all_gather(query_weight[layer_at], "fsdp", axis=0, tiled=True),
-            lax.all_gather(key_weight[layer_at], "fsdp", axis=0, tiled=True),
-            lax.all_gather(value_weight[layer_at], "fsdp", axis=0, tiled=True),
-            lax.all_gather(out_weight[layer_at], "fsdp", axis=0, tiled=True),
-            lax.all_gather(gate_weight[layer_at], "fsdp", axis=0, tiled=True),
-            lax.all_gather(up_weight[layer_at], "fsdp", axis=0, tiled=True),
-            lax.all_gather(down_weight[layer_at], "fsdp", axis=0, tiled=True),
-            lax.all_gather(norm_gains[layer_at], "fsdp", axis=1, tiled=True),
-            lax.all_gather(head_gains[layer_at], "fsdp", axis=1, tiled=True),
+            qkv_mat,
+            gathered(out_weight[layer_at]),
+            gathered(jnp.concatenate([gate_weight[layer_at], up_weight[layer_at]], 1)),
+            gathered(down_weight[layer_at]),
+            model_all[layer_at],
+            head_all[layer_at],
         )
         stream, retained = forward_layer(stream, weights_now, seg_own, seg_ext, cosine, sine_part)
         stored.append((weights_now, retained))
     output = stream.astype(jnp.bfloat16)
     upstream = cotangent[0].astype(jnp.float32)
     collected = [None] * layers
+    fsdp_at = lax.axis_index("fsdp")
     for layer_at in range(layers - 1, -1, -1):
         weights_now, retained = stored[layer_at]
-        weights_now = (
-            lax.all_gather(query_weight[layer_at], "fsdp", axis=0, tiled=True),
-            lax.all_gather(key_weight[layer_at], "fsdp", axis=0, tiled=True),
-            lax.all_gather(value_weight[layer_at], "fsdp", axis=0, tiled=True),
-            lax.all_gather(out_weight[layer_at], "fsdp", axis=0, tiled=True),
-            lax.all_gather(gate_weight[layer_at], "fsdp", axis=0, tiled=True),
-            lax.all_gather(up_weight[layer_at], "fsdp", axis=0, tiled=True),
-            lax.all_gather(down_weight[layer_at], "fsdp", axis=0, tiled=True),
-            lax.all_gather(norm_gains[layer_at], "fsdp", axis=1, tiled=True),
-            lax.all_gather(head_gains[layer_at], "fsdp", axis=1, tiled=True),
-        )
-        upstream, matrices, model_terms, head_terms = backward_layer(
+        upstream, shards, gain_sums = backward_layer(
             upstream, weights_now, retained, seg_own, seg_ext
         )
-        packed = pack_terms(matrices, model_terms, head_terms, fsdp_size)
-        groups = lax.axis_size("seq")
-        own_part = lax.psum_scatter(
-            packed.astype(jnp.bfloat16), "fsdp", scatter_dimension=0, tiled=True
-        ).astype(jnp.float32)
-        span_cols = own_part.shape[1] // groups
-        piece = lax.psum_scatter(
-            own_part.reshape(groups, span_cols), "seq", scatter_dimension=0, tiled=True
-        )
-        summed = (
-            lax.all_gather(piece.astype(jnp.bfloat16), "seq", axis=0, tiled=True)
-            .astype(piece.dtype)
-            .reshape(-1)
-        )
-        collected[layer_at] = unpack_terms(summed, matrices, model_terms, head_terms, fsdp_size)
+        model_width = 4 * fsdp_size * width
+        model_shard = lax.dynamic_slice_in_dim(
+            gain_sums[:model_width].reshape(4, -1), fsdp_at * width, width, 1
+        )
+        head_shard = lax.dynamic_slice_in_dim(
+            gain_sums[model_width:].reshape(2, -1), fsdp_at * head_width, head_width, 1
+        )
+        collected[layer_at] = (shards, model_shard, head_shard)
     input_grad = upstream.astype(jnp.bfloat16)
     stacked = [
         jnp.stack([collected[layer_at][0][number] for layer_at in range(layers)])

time: 1690 us -> 672 us (0.40)
  blocking collectives: 488 us -> 0 us
  waiting for transfers between devices: 570 us -> 305 us
  local copies, waits for them, and re-layouts: 251 us -> 53 us
  other arithmetic: 226 us -> 63.1 us
  starting transfers between devices: 43.5 us -> 146 us
    unnamed x1 -> x0, blocking collectives: 433 us -> none
    unnamed x14 -> x8, waiting for transfers between devices: 389 us -> 0.63 us
    ppermute x0 -> x74, waiting for transfers between devices: none -> 175 us  [swapped(): lax.ppermute(value, axis, [(source, source ^ bit) for source in range(cou...]
    convert_element_type x15 -> x53, other arithmetic: 127 us -> 23.3 us  [the longest x40 13.9 us: added(): (first_op.astype(jnp.float32) + second_op.astype(jnp.float32)).astype(jnp...]
    ppermute x0 -> x74, starting transfers between devices: none -> 97.9 us  [swapped(): lax.ppermute(value, axis, [(source, source ^ bit) for source in range(cou...]
    reshape x22 -> x10, local copies, waits for them, and re-layouts: 73.9 us -> 5.33 us  [the longest x2 2.06 us: query_piece(): raw_vals.reshape(tokens, HEADS, HD)]
    reshape x1 -> x0, other arithmetic: 64.6 us -> none  [local(): own_part.reshape(groups, span_cols)]
    all_gather x12 -> x8, waiting for transfers between devices: 180 us -> 123 us  [gathered(): return lax.all_gather(part, 'fsdp', axis=0, tiled=True)]
  transfers between devices with their start and end apart: 31 -> 100, of which waited for: 8 -> 58; matrix products, arithmetic and copies ran while one was open for 14% -> 22% of each run, Pallas kernels for 0% -> 0%
where the time goes in v1:
time: 672 us; the launch traced here: 666 us
  waiting for transfers between devices  305 us (45%)
  starting transfers between devices  146 us (22%)
  matrix products  80.6 us (12%)
  other arithmetic  63.1 us (9%)
  local copies, waits for them, and re-layouts  53 us (8%)
  between operations  18.4 us (3%)
    ppermute x74, waiting for transfers between devices, swapped(): lax.ppermute(value, axis, [(source, source ^ bit) for source in range(cou...  175 us
    all_gather x8, waiting for transfers between devices, gathered(): return lax.all_gather(part, 'fsdp', axis=0, tiled=True)  123 us
    ppermute x74, starting transfers between devices, swapped(): lax.ppermute(value, axis, [(source, source ^ bit) for source in range(cou...  97.9 us
    ppermute x18, starting transfers between devices, passed_along(): lax.ppermute(value, axis, [(source, source + steps) for source in range(f...  47.4 us
    dot_general x8, matrix products, outer_sum(): lax.dot_general(first_op, second_op, (((0,), (0,)), ((), ())), preferred_...  20.3 us
    unnamed x356, local copies, waits for them, and re-layouts  16.6 us
    dot_general x8, matrix products, back_dot(): lax.dot_general(first_op, second_op, (((1,), (1,)), ((), ())), preferred_...  16.4 us
    convert_element_type x40, other arithmetic, added(): (first_op.astype(jnp.float32) + second_op.astype(jnp.float32)).astype(jnp...  13.9 us
  transfers between devices with their start and end apart: 100, of which 58 were waited for; matrix products, arithmetic and copies ran while one was open for 22% of the time, Pallas kernels for 0%

profile of v1, /device:TPU:0, one launch (start us, length us, event | category | flops | bytes accessed | tf_op | source)
XLA Modules:
  0.0 665.9 jit_solution(5703842832867330117)
XLA Ops:
  20.4 4.9 collective-permute-start.3
  31.0 6.8 %all-gather.13.cloned.1.call-done = bf16[640,1548]{1,0:T(8,128)(2,1)} async-done(((bf16[160,1548]{1,0:T(8,128)(2,1)}), bf16[640,1548]{1,0:T(8,128)(2,1)}) %all-gather.13.cloned.1.call-update) | async-done | bytes 1981456 | tf_op jit(solution)/shard_map/all_gather | solution.py:352
  69.8 31.0 %all-gather.15.cloned.1.call-done = bf16[640,4096]{1,0:T(8,128)(2,1)} async-done(((bf16[160,4096]{1,0:T(8,128)(2,1)}), bf16[640,4096]{1,0:T(8,128)(2,1)}) %all-gather.15.cloned.1.call-update) | async-done | bytes 5242896 | tf_op jit(solution)/shard_map/all_gather | solution.py:352
  100.8 4.3 fusion.191
  108.0 20.4 %all-gather.23.cloned.1.call-done = bf16[1,2048,640]{2,1,0:T(8,128)(2,1)} async-done(((bf16[1,512,640]{2,1,0:T(8,128)(2,1)}), bf16[1,2048,640]{2,1,0:T(8,128)(2,1)}) %all-gather.23.cloned.1.call-update) | async-done | bytes 2621456 | tf_op jit(solution)/shard_map/all_gather | solution.py:352
  132.3 19.3 %all-gather.17.cloned.1.call-done = bf16[640,1536]{1,0:T(8,128)(2,1)} async-done(((bf16[160,1536]{1,0:T(8,128)(2,1)}), bf16[640,1536]{1,0:T(8,128)(2,1)}) %all-gather.17.cloned.1.call-update) | async-done | bytes 1966096 | tf_op jit(solution)/shard_map/all_gather | solution.py:352
  154.8 4.0 collective-permute-start.7
  164.9 4.0 collective-permute-start.9
  188.5 26.0 %all-gather.19.cloned.1.call-done = bf16[640,4096]{1,0:T(8,128)(2,1)} async-done(((bf16[160,4096]{1,0:T(8,128)(2,1)}), bf16[640,4096]{1,0:T(8,128)(2,1)}) %all-gather.19.cloned.1.call-update) | async-done | bytes 5242896 | tf_op jit(solution)/shard_map/all_gather | solution.py:352
  214.5 4.3 fusion.193
  222.5 19.7 %all-gather.27.cloned.1.call-done = bf16[1,2048,640]{2,1,0:T(8,128)(2,1)} async-done(((bf16[1,512,640]{2,1,0:T(8,128)(2,1)}), bf16[1,2048,640]{2,1,0:T(8,128)(2,1)}) %all-gather.27.cloned.1.call-update) | async-done | bytes 2621456 | tf_op jit(solution)/shard_map/all_gather | solution.py:352
  343.5 4.2 collective-permute-start.90
  349.4 5.4 collective-permute-start.91
  394.4 7.6 %collective-permute-done.43 = bf16[1,256,640]{2,1,0:T(8,128)(2,1)S(1)} collective-permute-done((bf16[1,256,640]{2,1,0:T(8,128)(2,1)S(1)}, bf16[1,256,640]{2,1,0:T(8,128)(2,1)S(1)}, u32[]{:S(2)}, u32[]{:S(2)}) %collective-permute-start.43) | collective-permute-done | bytes 327712 | tf_op jit(solution)/shard_map/ppermute | solution.py:22
  404.2 8.1 %collective-permute-done.35 = bf16[1,256,640]{2,1,0:T(8,128)(2,1)S(1)} collective-permute-done((bf16[1,256,640]{2,1,0:T(8,128)(2,1)S(1)}, bf16[1,256,640]{2,1,0:T(8,128)(2,1)S(1)}, u32[]{:S(2)}, u32[]{:S(2)}) %collective-permute-start.35) | collective-permute-done | bytes 327712 | tf_op jit(solution)/shard_map/ppermute | solution.py:22
  412.4 5.7 collective-permute-done.44
  428.3 5.7 collective-permute-done.36
  465.5 5.0 collective-permute-done.49
  471.6 4.9 collective-permute-done.41
  480.6 8.1 %collective-permute-done.28 = bf16[160,768]{1,0:T(8,128)(2,1)S(1)} collective-permute-done((bf16[160,768]{1,0:T(8,128)(2,1)S(1)}, bf16[160,768]{1,0:T(8,128)(2,1)S(1)}, u32[]{:S(2)}, u32[]{:S(2)}) %collective-permute-start.28) | collective-permute-done | bytes 245792 | tf_op jit(solution)/shard_map/ppermute | solution.py:22
  490.7 4.4 collective-permute-done.29
  522.8 5.8 collective-permute-done.23
  530.9 4.7 collective-permute-done.24
  537.1 4.6 collective-permute-done.77
  570.7 4.3 collective-permute-start.73
  580.3 11.6 %collective-permute-done.51 = bf16[1,160,4096]{2,1,0:T(8,128)(2,1)S(1)} collective-permute-done((bf16[1,160,4096]{2,1,0:T(8,128)(2,1)S(1)}, bf16[1,160,4096]{2,1,0:T(8,128)(2,1)S(1)}, u32[]{:S(2)}, u32[]{:S(2)}) %collective-permute-start.51) | collective-permute-done | bytes 1310752 | tf_op jit(solution)/shard_map/ppermute | solution.py:22
  597.3 5.7 collective-permute-done.52
  606.3 10.5 %collective-permute-done.53 = bf16[160,1024]{1,0:T(8,128)(2,1)S(1)} collective-permute-done((bf16[160,1024]{1,0:T(8,128)(2,1)S(1)}, bf16[160,1024]{1,0:T(8,128)(2,1)S(1)}, u32[]{:S(2)}, u32[]{:S(2)}) %collective-permute-start.53) | collective-permute-done | bytes 327712 | tf_op jit(solution)/shard_map/ppermute | solution.py:22
  620.0 6.1 collective-permute-done.54
  628.9 4.5 collective-permute-done.55
  642.3 5.3 collective-permute-done.65
  648.4 6.2 collective-permute-done.57
  (853 shorter events, 374.1 us)
Async XLA Ops:
  7.2 30.6 %all-gather.13.cloned.1.call-start = ((), (), s32[]{:S(2)}) async-start(), calls=%async_computation | async-start | bytes 2662400 | tf_op jit(solution)/shard_map/all_gather | solution.py:352
  12.2 54.1 %all-gather.21.cloned.1.call-start = ((), (), s32[]{:S(2)}) async-start(), calls=%async_computation.4 | async-start | bytes 1638400 | tf_op jit(solution)/shard_map/all_gather | solution.py:352
  13.1 87.6 %all-gather.15.cloned.1.call-start = ((), (), s32[]{:S(2)}) async-start(), calls=%async_computation.1 | async-start | bytes 6553600 | tf_op jit(solution)/shard_map/all_gather | solution.py:352
  15.9 112.5 %all-gather.23.cloned.1.call-start = ((), (), s32[]{:S(2)}) async-start(), calls=%async_computation.5 | async-start | bytes 3276800 | tf_op jit(solution)/shard_map/all_gather | solution.py:352
  17.7 134.0 %all-gather.17.cloned.1.call-start = ((), (), s32[]{:S(2)}) async-start(), calls=%async_computation.2 | async-start | bytes 2457600 | tf_op jit(solution)/shard_map/all_gather | solution.py:352
  18.6 165.4 %all-gather.25.cloned.1.call-start = ((), (), s32[]{:S(2)}) async-start(), calls=%async_computation.6 | async-start | bytes 1638400 | tf_op jit(solution)/shard_map/all_gather | solution.py:352
  19.1 195.4 %all-gather.19.cloned.1.call-start = ((), (), s32[]{:S(2)}) async-start(), calls=%async_computation.3 | async-start | bytes 6553600 | tf_op jit(solution)/shard_map/all_gather | solution.py:352
  20.4 221.9 %all-gather.27.cloned.1.call-start = ((), (), s32[]{:S(2)}) async-start(), calls=%async_computation.7 | async-start | bytes 3276800 | tf_op jit(solution)/shard_map/all_gather | solution.py:352
  42.3 20.6 %collective-permute-start.1 = (bf16[256,256]{1,0:T(8,128)(2,1)}, bf16[256,256]{1,0:T(8,128)(2,1)}, u32[]{:S(2)}, u32[]{:S(2)}) collective-permute-start(bf16[256,256]{1,0:T(8,128)(2,1)} %slice.681), channel_id=1, source_target_pairs={{0,4},{4,8},{8,12},{12,16},{16,20},{20,24},{24,28},{1,5},{5,9},{9,... | collective-permute-start | bytes 393224 | tf_op jit(solution)/shard_map/ppermute | solution.py:17
  46.3 16.6 %collective-permute-start = (bf16[256,256]{1,0:T(8,128)(2,1)}, bf16[256,256]{1,0:T(8,128)(2,1)}, u32[]{:S(2)}, u32[]{:S(2)}) collective-permute-start(bf16[256,256]{1,0:T(8,128)(2,1)} %slice.681), channel_id=1, source_target_pairs={{0,8},{4,12},{8,16},{12,20},{16,24},{20,28},{1,9},{5,13},{9,17},{1... | collective-permute-start | bytes 393224 | tf_op jit(solution)/shard_map/ppermute | solution.py:17
  154.8 25.8 %collective-permute-start.7 = (bf16[256,256]{1,0:T(8,128)(2,1)}, bf16[256,256]{1,0:T(8,128)(2,1)}, u32[]{:S(2)}, u32[]{:S(2)}) collective-permute-start(bf16[256,256]{1,0:T(8,128)(2,1)} %slice.680), channel_id=1, source_target_pairs={{0,4},{4,8},{8,12},{12,16},{16,20},{20,24},{24,28},{1,5},{5,9},{9,... | collective-permute-start | bytes 393224 | tf_op jit(solution)/shard_map/ppermute | solution.py:17
  158.8 21.8 %collective-permute-start.6 = (bf16[256,256]{1,0:T(8,128)(2,1)}, bf16[256,256]{1,0:T(8,128)(2,1)}, u32[]{:S(2)}, u32[]{:S(2)}) collective-permute-start(bf16[256,256]{1,0:T(8,128)(2,1)} %slice.680), channel_id=1, source_target_pairs={{0,8},{4,12},{8,16},{12,20},{16,24},{20,28},{1,9},{5,13},{9,17},{1... | collective-permute-start | bytes 393224 | tf_op jit(solution)/shard_map/ppermute | solution.py:17
  269.6 26.8 %collective-permute-start.13 = (bf16[256,256]{0,1:T(8,128)(2,1)}, bf16[256,256]{0,1:T(8,128)(2,1)}, u32[]{:S(2)}, u32[]{:S(2)}) collective-permute-start(bf16[256,256]{0,1:T(8,128)(2,1)} %get-tuple-element.347), channel_id=1, source_target_pairs={{4,0},{8,4},{12,8},{16,12},{20,16},{24,20},{28,24},{5,1},{9,5},{13... | collective-permute-start | bytes 393224 | tf_op jit(solution)/shard_map/ppermute | solution.py:17
  270.9 25.5 %collective-permute-start.12 = (bf16[256,256]{0,1:T(8,128)(2,1)}, bf16[256,256]{0,1:T(8,128)(2,1)}, u32[]{:S(2)}, u32[]{:S(2)}) collective-permute-start(bf16[256,256]{0,1:T(8,128)(2,1)} %get-tuple-element.346), channel_id=1, source_target_pairs={{8,0},{12,4},{16,8},{20,12},{24,16},{28,20},{9,1},{13,5},{17,9},{2... | collective-permute-start | bytes 393224 | tf_op jit(solution)/shard_map/ppermute | solution.py:17
  286.4 104.1 %collective-permute-start.42 = (bf16[2,256,640]{2,1,0:T(8,128)(2,1)}, bf16[2,256,640]{2,1,0:T(8,128)(2,1)}, u32[]{:S(2)}, u32[]{:S(2)}) collective-permute-start(bf16[2,256,640]{2,1,0:T(8,128)(2,1)} %dynamic-slice_bitcast_fusion.8), channel_id=1, source_target_pairs={{0,1},{1,0},{2,3},{3,2},{4,5},{5,4},{6,7},{7,6},{8,9},{9,8},{10,11... | collective-permute-start | bytes 1966088 | tf_op jit(solution)/shard_map/ppermute | solution.py:22
  291.6 262.5 %collective-permute-start.58 = (bf16[2,160,4096]{2,1,0:T(8,128)(2,1)}, bf16[2,160,4096]{2,1,0:T(8,128)(2,1)}, u32[]{:S(2)}, u32[]{:S(2)}) collective-permute-start(bf16[2,160,4096]{2,1,0:T(8,128)(2,1)} %dynamic-slice_bitcast_fusion), channel_id=1, source_target_pairs={{0,1},{1,0},{2,3},{3,2},{4,5},{5,4},{6,7},{7,6},{8,9},{9,8},{10,11... | collective-permute-start | bytes 7864328 | tf_op jit(solution)/shard_map/ppermute | solution.py:22
  327.6 28.9 %collective-permute-start.15 = (bf16[256,256]{1,0:T(8,128)(2,1)}, bf16[256,256]{1,0:T(8,128)(2,1)}, u32[]{:S(2)}, u32[]{:S(2)}) collective-permute-start(bf16[256,256]{1,0:T(8,128)(2,1)} %get-tuple-element.341), channel_id=1, source_target_pairs={{4,0},{8,4},{12,8},{16,12},{20,16},{24,20},{28,24},{5,1},{9,5},{13... | collective-permute-start | bytes 393224 | tf_op jit(solution)/shard_map/ppermute | solution.py:17
  334.6 23.3 %collective-permute-start.14 = (bf16[256,256]{1,0:T(8,128)(2,1)}, bf16[256,256]{1,0:T(8,128)(2,1)S(1)}, u32[]{:S(2)}, u32[]{:S(2)}) collective-permute-start(bf16[256,256]{1,0:T(8,128)(2,1)} %get-tuple-element.340), channel_id=1, source_target_pairs={{8,0},{12,4},{16,8},{20,12},{24,16},{28,20},{9,1},{13,5},{17,9},{2... | collective-permute-start | bytes 393224 | tf_op jit(solution)/shard_map/ppermute | solution.py:17
  356.4 78.1 %collective-permute-start.74 = (bf16[2,512,640]{2,1,0:T(8,128)(2,1)}, bf16[2,512,640]{2,1,0:T(8,128)(2,1)}, u32[]{:S(2)}, u32[]{:S(2)}) collective-permute-start(bf16[2,512,640]{2,1,0:T(8,128)(2,1)} %dynamic-slice_bitcast_fusion.2), channel_id=1, source_target_pairs={{0,1},{1,0},{2,3},{3,2},{4,5},{5,4},{6,7},{7,6},{8,9},{9,8},{10,11... | collective-permute-start | bytes 3932168 | tf_op jit(solution)/shard_map/ppermute | solution.py:22
  364.5 37.6 %collective-permute-start.26 = (bf16[2,160,1536]{2,1,0:T(8,128)(2,1)}, bf16[2,160,1536]{2,1,0:T(8,128)(2,1)}, u32[]{:S(2)}, u32[]{:S(2)}) collective-permute-start(bf16[2,160,1536]{2,1,0:T(8,128)(2,1)} %dynamic-slice_bitcast_fusion.4), channel_id=1, source_target_pairs={{0,1},{1,0},{2,3},{3,2},{4,5},{5,4},{6,7},{7,6},{8,9},{9,8},{10,11... | collective-permute-start | bytes 2949128 | tf_op jit(solution)/shard_map/ppermute | solution.py:22
  390.5 170.5 %collective-permute-start.50 = (bf16[2,160,4096]{2,1,0:T(8,128)(2,1)}, bf16[2,160,4096]{2,1,0:T(8,128)(2,1)S(1)}, u32[]{:S(2)}, u32[]{:S(2)}) collective-permute-start(bf16[2,160,4096]{2,1,0:T(8,128)(2,1)} %dynamic-slice_bitcast_fusion.1), channel_id=1, source_target_pairs={{0,1},{1,0},{2,3},{3,2},{4,5},{5,4},{6,7},{7,6},{8,9},{9,8},{10,11... | collective-permute-start | bytes 7864328 | tf_op jit(solution)/shard_map/ppermute | solution.py:22
  402.0 20.8 %collective-permute-start.18 = (bf16[2,160,1536]{2,1,0:T(8,128)(2,1)S(1)}, bf16[2,160,1536]{2,1,0:T(8,128)(2,1)S(1)}, u32[]{:S(2)}, u32[]{:S(2)}) collective-permute-start(bf16[2,160,1536]{2,1,0:T(8,128)(2,1)S(1)} %copy-done.59), channel_id=1, source_target_pairs={{0,1},{1,0},{2,3},{3,2},{4,5},{5,4},{6,7},{7,6},{8,9},{9,8},{10,11... | collective-permute-start | bytes 2949128 | tf_op jit(solution)/shard_map/ppermute | solution.py:22
  422.8 37.9 %collective-permute-start.66 = (bf16[2,512,640]{2,1,0:T(8,128)(2,1)S(1)}, bf16[2,512,640]{2,1,0:T(8,128)(2,1)S(1)}, u32[]{:S(2)}, u32[]{:S(2)}) collective-permute-start(bf16[2,512,640]{2,1,0:T(8,128)(2,1)S(1)} %copy-done.50), channel_id=1, source_target_pairs={{0,1},{1,0},{2,3},{3,2},{4,5},{5,4},{6,7},{7,6},{8,9},{9,8},{10,11... | collective-permute-start | bytes 3932168 | tf_op jit(solution)/shard_map/ppermute | solution.py:22
  434.1 37.0 %collective-permute-start.27 = (bf16[1,160,1536]{2,1,0:T(8,128)(2,1)S(1)}, bf16[1,160,1536]{2,1,0:T(8,128)(2,1)S(1)}, u32[]{:S(2)}, u32[]{:S(2)}) collective-permute-start(bf16[1,160,1536]{2,1,0:T(8,128)(2,1)S(1)} %constant_dynamic-slice_fusion.24), channel_id=1, source_target_pairs={{0,2},{1,3},{2,0},{3,1},{4,6},{5,7},{6,4},{7,5},{8,10},{9,11},{10,... | collective-permute-start | bytes 1474568 | tf_op jit(solution)/shard_map/ppermute | solution.py:22
  459.1 21.0 %collective-permute-start.19 = (bf16[1,160,1536]{2,1,0:T(8,128)(2,1)S(1)}, bf16[1,160,1536]{2,1,0:T(8,128)(2,1)S(1)}, u32[]{:S(2)}, u32[]{:S(2)}) collective-permute-start(bf16[1,160,1536]{2,1,0:T(8,128)(2,1)S(1)} %constant_dynamic-slice_fusion.27), channel_id=1, source_target_pairs={{0,2},{1,3},{2,0},{3,1},{4,6},{5,7},{6,4},{7,5},{8,10},{9,11},{10,... | collective-permute-start | bytes 1474568 | tf_op jit(solution)/shard_map/ppermute | solution.py:22
  470.5 18.6 %collective-permute-start.75 = (bf16[1,512,640]{2,1,0:T(8,128)(2,1)S(1)}, bf16[1,512,640]{2,1,0:T(8,128)(2,1)S(1)}, u32[]{:S(2)}, u32[]{:S(2)}) collective-permute-start(bf16[1,512,640]{2,1,0:T(8,128)(2,1)S(1)} %constant_dynamic-slice_fusion.6), channel_id=1, source_target_pairs={{0,2},{1,3},{2,0},{3,1},{4,6},{5,7},{6,4},{7,5},{8,10},{9,11},{10,... | collective-permute-start | bytes 1966088 | tf_op jit(solution)/shard_map/ppermute | solution.py:22
  476.5 33.1 %collective-permute-start.67 = (bf16[1,512,640]{2,1,0:T(8,128)(2,1)S(1)}, bf16[1,512,640]{2,1,0:T(8,128)(2,1)S(1)}, u32[]{:S(2)}, u32[]{:S(2)}) collective-permute-start(bf16[1,512,640]{2,1,0:T(8,128)(2,1)S(1)} %constant_dynamic-slice_fusion.9), channel_id=1, source_target_pairs={{0,2},{1,3},{2,0},{3,1},{4,6},{5,7},{6,4},{7,5},{8,10},{9,11},{10,... | collective-permute-start | bytes 1966088 | tf_op jit(solution)/shard_map/ppermute | solution.py:22
  495.1 35.6 %collective-permute-start.76 = (bf16[256,640]{1,0:T(8,128)(2,1)S(1)}, bf16[256,640]{1,0:T(8,128)(2,1)S(1)}, u32[]{:S(2)}, u32[]{:S(2)}) collective-permute-start(bf16[256,640]{1,0:T(8,128)(2,1)S(1)} %dynamic-slice_bitcast_fusion.10), channel_id=1, source_target_pairs={{0,4},{4,0},{8,12},{12,8},{16,20},{20,16},{24,28},{28,24},{1,5},{5... | collective-permute-start | bytes 983048 | tf_op jit(solution)/shard_map/ppermute | solution.py:22
  519.0 16.8 %collective-permute-start.68 = (bf16[256,640]{1,0:T(8,128)(2,1)S(1)}, bf16[256,640]{1,0:T(8,128)(2,1)S(1)}, u32[]{:S(2)}, u32[]{:S(2)}) collective-permute-start(bf16[256,640]{1,0:T(8,128)(2,1)S(1)} %dynamic-slice_bitcast_fusion.11), channel_id=1, source_target_pairs={{0,4},{4,0},{8,12},{12,8},{16,20},{20,16},{24,28},{28,24},{1,5},{5... | collective-permute-start | bytes 983048 | tf_op jit(solution)/shard_map/ppermute | solution.py:22
  557.4 20.5 %collective-permute-start.59 = (bf16[1,160,4096]{2,1,0:T(8,128)(2,1)S(1)}, bf16[1,160,4096]{2,1,0:T(8,128)(2,1)S(1)}, u32[]{:S(2)}, u32[]{:S(2)}) collective-permute-start(bf16[1,160,4096]{2,1,0:T(8,128)(2,1)S(1)} %constant_dynamic-slice_fusion.12), channel_id=1, source_target_pairs={{0,2},{1,3},{2,0},{3,1},{4,6},{5,7},{6,4},{7,5},{8,10},{9,11},{10,... | collective-permute-start | bytes 3932168 | tf_op jit(solution)/shard_map/ppermute | solution.py:22
  562.2 29.8 %collective-permute-start.51 = (bf16[1,160,4096]{2,1,0:T(8,128)(2,1)S(1)}, bf16[1,160,4096]{2,1,0:T(8,128)(2,1)S(1)}, u32[]{:S(2)}, u32[]{:S(2)}) collective-permute-start(bf16[1,160,4096]{2,1,0:T(8,128)(2,1)S(1)} %constant_dynamic-slice_fusion.15), channel_id=1, source_target_pairs={{0,2},{1,3},{2,0},{3,1},{4,6},{5,7},{6,4},{7,5},{8,10},{9,11},{10,... | collective-permute-start | bytes 3932168 | tf_op jit(solution)/shard_map/ppermute | solution.py:22
  570.7 23.6 %collective-permute-start.73 = (bf16[256,640]{1,0:T(8,128)(2,1)S(1)}, bf16[256,640]{1,0:T(8,128)(2,1)S(1)}, u32[]{:S(2)}, u32[]{:S(2)}) collective-permute-start(bf16[256,640]{1,0:T(8,128)(2,1)S(1)} %pad_maximum_fusion.26), channel_id=1, source_target_pairs={{0,4},{4,0},{8,12},{12,8},{16,20},{20,16},{24,28},{28,24},{1,5},{5... | collective-permute-start | bytes 983048 | tf_op jit(solution)/shard_map/ppermute | solution.py:22
  (241 other events, 1831.9 us)
Sparse Core Ops, SparseCore 0:
  12.3 25.4 all-gather.12
  39.9 18.1 all-gather.20
  60.3 40.4 all-gather.14
  102.8 25.5 all-gather.22
  129.8 21.8 all-gather.16
  153.7 18.1 all-gather.24
  174.0 40.4 all-gather.18
  216.7 25.5 all-gather.26

commit v2 on v1

--- a/solution.py
+++ b/solution.py
@@ -1,11 +1,16 @@
+import functools
+
 import jax
 import jax.numpy as jnp
 from jax import lax
+from jax.experimental import pallas as pl
+from jax.experimental.pallas import tpu as pltpu
 from jax.sharding import PartitionSpec as P
 
 HEADS = 4
 HD = 256
 WINDOW = 512
+VMEM_MIB = 58
 
 
 EPS = 1e-06
@@ -65,11 +70,144 @@
     return part.astype(jnp.float32)
 
 
-def summed_everywhere(values):
-    for axis in ("fsdp", "seq"):
-        for bit in axis_bits(axis):
-            values = values + swapped(values, axis, bit)
-    return values
+def part_of(ref, dim, begin_at, size):
+    if dim == 0:
+        return ref.at[pl.ds(pl.multiple_of(begin_at, 16), size), :]
+    return ref.at[:, pl.ds(pl.multiple_of(begin_at, 128), size)]
+
+
+def add_into(target, first_op, second_op):
+    step = 32
+
+    def body(number, carry):
+        rows = pl.ds(pl.multiple_of(number * step, step), step)
+        target[rows, :] = (
+            first_op[rows, :].astype(jnp.float32) + second_op[rows, :].astype(jnp.float32)
+        ).astype(jnp.bfloat16)
+        return carry
+
+    lax.fori_loop(0, target.shape[0] // step, body, 0)
+
+
+def reduce_kernel(dims, bits, *refs):
+    count = len(dims)
+    levels = len(bits)
+    terms, sums = refs[:count], refs[count : 2 * count]
+    refs = refs[2 * count :]
+    halves, shards = refs[:count], refs[count : 2 * count]
+    slots = refs[2 * count : (2 + levels) * count]
+    send_sem, recv_sem = refs[-2:]
+    at_f = lax.axis_index("fsdp")
+    at_s = lax.axis_index("seq")
+    core, far = at_f % 2, at_f // 2
+    core_peer = {"fsdp": at_f + 1 - 2 * core}
+    far_peer = {"fsdp": at_f + 2 - 4 * far}
+    mine = [(at_s // bit) % 2 for bit in bits]
+    seq_peers = [{"seq": at_s + bit - 2 * bit * one} for bit, one in zip(bits, mine)]
+    barrier = pltpu.get_barrier_semaphore()
+    for peer in [core_peer, far_peer] + seq_peers:
+        pl.semaphore_signal(barrier, inc=1, device_id=peer, device_id_type=pl.DeviceIdType.MESH)
+    pl.semaphore_wait(barrier, 2 + levels)
+
+    stages = 2 + 2 * levels
+    flying = {}
+
+    def offset(group, level):
+        size = shards[group].shape[dims[group]]
+        total = 0
+        for done in range(level):
+            size = size // 2
+            total = total + mine[done] * size
+        return total, size
+
+    def send(group, stage, source, target, peer):
+        copy = pltpu.make_async_remote_copy(
+            src_ref=source,
+            dst_ref=target,
+            send_sem=send_sem.at[group, stage],
+            recv_sem=recv_sem.at[group, stage],
+            device_id=peer,
+            device_id_type=pl.DeviceIdType.MESH,
+        )
+        copy.start()
+        flying[group] = copy
+
+    def begin(group, stage):
+        dim = dims[group]
+        if stage == 0:
+            send(group, stage, terms[group].at[:, 1 - core], halves[group], core_peer)
+        elif stage == 1:
+            send(group, stage, halves[group].at[1 - far], shards[group], far_peer)
+        elif stage < 2 + levels:
+            level = stage - 2
+            start, size = offset(group, level)
+            half = size // 2
+            source = part_of(shards[group], dim, start + (1 - mine[level]) * half, half)
+            send(group, stage, source, slots[level * count + group], seq_peers[level])
+        else:
+            level = stages - 1 - stage
+            start, size = offset(group, level + 1)
+            piece = part_of(sums[group], dim, start, size)
+            send(group, stage, piece, piece, seq_peers[level])
+
+    def finish(group, stage):
+        dim = dims[group]
+        flying[group].wait()
+        if stage == 0:
+            for number in range(2):
+                half = halves[group].at[number]
+                add_into(half, terms[group].at[number, core], half)
+        elif stage == 1:
+            add_into(shards[group], halves[group].at[far], shards[group])
+        elif stage < 2 + levels:
+            level = stage - 2
+            start, size = offset(group, level + 1)
+            kept = part_of(shards[group], dim, start, size)
+            target = part_of(sums[group], dim, start, size) if level == levels - 1 else kept
+            add_into(target, kept, slots[level * count + group])
+
+    for tick in range(count + stages):
+        for group in reversed(range(count)):
+            stage = tick - group
+            if 1 <= stage <= stages:
+                finish(group, stage - 1)
+            if 0 <= stage < stages:
+                begin(group, stage)
+
+
+def summed_shards(terms):
+    fsdp_size, seq_size = lax.axis_size("fsdp"), lax.axis_size("seq")
+    dims = []
+    for term in terms:
+        rows, cols = term.shape[0] // fsdp_size, term.shape[1]
+        if rows % (32 * seq_size) == 0:
+            dims.append(0)
+        elif rows % 32 == 0 and cols % (128 * seq_size) == 0:
+            dims.append(1)
+    if fsdp_size != 4 or len(dims) < len(terms):
+        return [summed_shard(term) for term in terms]
+    bits = axis_bits("seq")
+    views = [term.reshape(2, 2, term.shape[0] // 4, term.shape[1]) for term in terms]
+    shapes = [view.shape[2:] for view in views]
+    scratch = [pltpu.VMEM((2,) + shape, jnp.bfloat16) for shape in shapes]
+    scratch += [pltpu.VMEM(shape, jnp.bfloat16) for shape in shapes]
+    for bit in bits:
+        for (rows, cols), dim in zip(shapes, dims):
+            piece = (rows // (2 * bit), cols) if dim == 0 else (rows, cols // (2 * bit))
+            scratch.append(pltpu.VMEM(piece, jnp.bfloat16))
+    flights = (len(terms), 2 + 2 * len(bits))
+    scratch += [pltpu.SemaphoreType.DMA(flights), pltpu.SemaphoreType.DMA(flights)]
+    sums = pl.pallas_call(
+        functools.partial(reduce_kernel, tuple(dims), tuple(bits)),
+        out_shape=[jax.ShapeDtypeStruct(shape, jnp.bfloat16) for shape in shapes],
+        in_specs=[pl.BlockSpec(memory_space=pltpu.VMEM)] * len(terms),
+        out_specs=[pl.BlockSpec(memory_space=pltpu.VMEM)] * len(terms),
+        scratch_shapes=scratch,
+        compiler_params=pltpu.CompilerParams(
+            collective_id=0, has_side_effects=True, vmem_limit_bytes=VMEM_MIB * 2**20
+        ),
+    )(*views)
+    return [value.astype(jnp.float32) for value in sums]
 
 
 def rms_scale(values, gain_vec):
@@ -160,9 +298,9 @@
     key_parts = []
     value_parts = []
     for shift_by, rim_rows in rim_sizes(tokens):
-        got_key, got_value = passed_along((key_low, values), "seq", shift_by)
-        key_parts.append(got_key)
-        value_parts.append(got_value)
+        got_both = passed_along(jnp.concatenate([key_low, values], 1), "seq", shift_by)
+        key_parts.append(got_both[:, :HD])
+        value_parts.append(got_both[:, HD:])
     key_ext = jnp.concatenate(key_parts + [key_low], 0)
     value_ext = jnp.concatenate(value_parts + [values], 0)
     scores, allowed = block_scores(query_low, key_ext, seg_own, seg_ext)
@@ -232,17 +370,20 @@
     block_rows = min(512, tokens)
     grad_ffn, gain_ffn = pull_ffn(upstream)
     ffn_low = grad_ffn.astype(jnp.bfloat16)
-    down_grad = summed_shard(outer_sum(act_low, ffn_low).astype(jnp.bfloat16))
+    down_term = outer_sum(act_low, ffn_low).astype(jnp.bfloat16)
     grad_act = back_dot(ffn_low, down_mat)
     grad_gate, grad_up = pull_act(grad_act)
-    both_low = jnp.concatenate([grad_gate, grad_up], 1).astype(jnp.bfloat16)
-    both_grad = summed_shard(outer_sum(hidden_two, both_low).astype(jnp.bfloat16))
+    gate_low = grad_gate.astype(jnp.bfloat16)
+    up_low = grad_up.astype(jnp.bfloat16)
+    both_low = jnp.concatenate([gate_low, up_low], 1)
+    gate_term = outer_sum(hidden_two, gate_low).astype(jnp.bfloat16)
+    up_term = outer_sum(hidden_two, up_low).astype(jnp.bfloat16)
     grad_hidden_two = back_dot(both_low, both_mat)
     middle_part, gain_pre = pull_pre(grad_hidden_two)
     grad_middle = upstream + middle_part
     grad_proj, gain_post = pull_post(grad_middle)
     proj_low = grad_proj.astype(jnp.bfloat16)
-    out_grad = summed_shard(outer_sum(attended, proj_low).astype(jnp.bfloat16))
+    out_term = outer_sum(attended, proj_low).astype(jnp.bfloat16)
     grad_att = back_dot(proj_low, out_mat).astype(jnp.bfloat16).reshape(tokens, HEADS, HD)
     key_back = jnp.zeros(key_ext.shape, jnp.float32)
     value_back = jnp.zeros(value_ext.shape, jnp.float32)
@@ -274,14 +415,11 @@
     value_own = value_back[WINDOW:]
     offset = 0
     for shift_by, rim_rows in rim_sizes(tokens):
-        got_key, got_value = (
-            passed_along(
-                key_back[offset : offset + rim_rows].astype(jnp.bfloat16), "seq", -shift_by
-            ).astype(jnp.float32),
-            passed_along(
-                value_back[offset : offset + rim_rows].astype(jnp.bfloat16), "seq", -shift_by
-            ).astype(jnp.float32),
-        )
+        backs = (key_back[offset : offset + rim_rows], value_back[offset : offset + rim_rows])
+        got_both = passed_along(
+            jnp.concatenate(backs, 1).astype(jnp.bfloat16), "seq", -shift_by
+        ).astype(jnp.float32)
+        got_key, got_value = got_both[:, :HD], got_both[:, HD:]
         key_own = key_own.at[tokens - rim_rows :].add(got_key)
         value_own = value_own.at[tokens - rim_rows :].add(got_value)
         offset = offset + rim_rows
@@ -295,22 +433,44 @@
         ],
         1,
     )
-    qkv_grad = summed_shard(outer_sum(hidden, qkv_low).astype(jnp.bfloat16))
+    qkv_term = outer_sum(hidden, qkv_low).astype(jnp.bfloat16)
     grad_hidden = back_dot(qkv_low, qkv_mat)
     grad_input, gain_in = pull_in(grad_hidden)
-    gain_terms = jnp.concatenate([gain_in, gain_post, gain_pre, gain_ffn, gain_query, gain_key])
+    fsdp_size = lax.axis_size("fsdp")
+    width = qkv_term.shape[0] // fsdp_size
+    head_terms = jnp.stack([gain_query, gain_key]).T.reshape(fsdp_size, -1, 2)
+    head_terms = jnp.pad(head_terms, ((0, 0), (0, width - head_terms.shape[1]), (0, 0)))
+    gain_terms = jnp.concatenate(
+        [
+            jnp.stack([gain_in, gain_post, gain_pre, gain_ffn]).T,
+            head_terms.reshape(fsdp_size * width, 2),
+        ],
+        1,
+    ).astype(jnp.bfloat16)
+    used = qkv_term.shape[1] + 6
+    padding = -used % 1024
+    qkv_term = jnp.concatenate(
+        [qkv_term, gain_terms, jnp.zeros((fsdp_size * width, padding), jnp.bfloat16)], 1
+    )
+    return (grad_middle + grad_input, [gate_term, up_term, down_term, qkv_term, out_term])
+
+
+def split_sums(sums, head_width):
+    gate_grad, up_grad, down_grad, qkv_grad, out_grad = sums
     query_cols = HEADS * HD
-    ffn_cols = both_grad.shape[1] // 2
+    gain_at = query_cols + 2 * HD
     shards = (
         qkv_grad[:, :query_cols],
         qkv_grad[:, query_cols : query_cols + HD],
-        qkv_grad[:, query_cols + HD :],
+        qkv_grad[:, query_cols + HD : gain_at],
         out_grad,
-        both_grad[:, :ffn_cols],
-        both_grad[:, ffn_cols:],
+        gate_grad,
+        up_grad,
         down_grad,
     )
-    return (grad_middle + grad_input, shards, summed_everywhere(gain_terms))
+    model_shard = qkv_grad[:, gain_at : gain_at + 4].T
+    head_shard = qkv_grad[:head_width, gain_at + 4 : gain_at + 6].T
+    return (shards, model_shard, head_shard)
 
 
 def local(
@@ -376,20 +536,15 @@
     output = stream.astype(jnp.bfloat16)
     upstream = cotangent[0].astype(jnp.float32)
     collected = [None] * layers
-    fsdp_at = lax.axis_index("fsdp")
+    all_terms = []
     for layer_at in range(layers - 1, -1, -1):
         weights_now, retained = stored[layer_at]
-        upstream, shards, gain_sums = backward_layer(
-            upstream, weights_now, retained, seg_own, seg_ext
-        )
-        model_width = 4 * fsdp_size * width
-        model_shard = lax.dynamic_slice_in_dim(
-            gain_sums[:model_width].reshape(4, -1), fsdp_at * width, width, 1
-        )
-        head_shard = lax.dynamic_slice_in_dim(
-            gain_sums[model_width:].reshape(2, -1), fsdp_at * head_width, head_width, 1
-        )
-        collected[layer_at] = (shards, model_shard, head_shard)
+        upstream, terms = backward_layer(upstream, weights_now, retained, seg_own, seg_ext)
+        all_terms.extend(terms)
+    sums = summed_shards(all_terms)
+    for layer_at in range(layers):
+        from_at = (layers - 1 - layer_at) * len(terms)
+        collected[layer_at] = split_sums(sums[from_at : from_at + len(terms)], head_width)
     input_grad = upstream.astype(jnp.bfloat16)
     stacked = [
         jnp.stack([collected[layer_at][0][number] for layer_at in range(layers)])

time: 672 us -> 589 us (0.88)
  Pallas kernels: 0 us -> 198 us
  waiting for transfers between devices: 305 us -> 136 us
  starting transfers between devices: 146 us -> 29.7 us
  local copies, waits for them, and re-layouts: 53 us -> 62.7 us
    pallas_call x0 -> x1, Pallas kernels: none -> 198 us  [summed_shards(): pl.pallas_call(functools.partial(reduce_kernel, tuple(dims), tuple(bits))...]
    ppermute x74 -> x0, waiting for transfers between devices: 175 us -> none  [swapped(): lax.ppermute(value, axis, [(source, source ^ bit) for source in range(cou...]
    ppermute x74 -> x0, starting transfers between devices: 97.9 us -> none  [swapped(): lax.ppermute(value, axis, [(source, source ^ bit) for source in range(cou...]
    ppermute x18 -> x10, starting transfers between devices: 47.4 us -> 29.4 us  [passed_along(): lax.ppermute(value, axis, [(source, source + steps) for source in range(f...]
    squeeze x16 -> x0, local copies, waits for them, and re-layouts: 12.4 us -> none  [chosen(): return lax.dynamic_index_in_dim(value, at, dim, keepdims=False)]
    convert_element_type x46 -> x8, other arithmetic: 16.9 us -> 4.49 us  [the longest x4 2.1 us: backward_layer(): got_both = passed_along(jnp.concatenate(backs, 1).astype(jnp.bfloat16), '...]
    concatenate x2, local copies, waits for them, and re-layouts: 0.01 us -> 8.92 us  [backward_layer(): jnp.concatenate([qkv_term, gain_terms, jnp.zeros((fsdp_size * width, padd...]
    dot_general x8 -> x10, matrix products: 20.3 us -> 23.1 us  [outer_sum(): lax.dot_general(first_op, second_op, (((0,), (0,)), ((), ())), preferred_...]
  transfers between devices with their start and end apart: 100 -> 18, of which waited for: 58 -> 10; matrix products, arithmetic and copies ran while one was open for 22% -> 15% of each run, Pallas kernels for 0% -> 0%
where the time goes in v2:
time: 589 us; the launch traced here: 584 us
  Pallas kernels  198 us (34%)
  waiting for transfers between devices  136 us (23%)
  matrix products  79.1 us (13%)
  local copies, waits for them, and re-layouts  62.7 us (11%)
  other arithmetic  60.5 us (10%)
  starting transfers between devices  29.7 us (5%)
  between operations  17.3 us (3%)
    pallas_call x1, Pallas kernels, summed_shards(): pl.pallas_call(functools.partial(reduce_kernel, tuple(dims), tuple(bits))...  198 us
    all_gather x8, waiting for transfers between devices, gathered(): return lax.all_gather(part, 'fsdp', axis=0, tiled=True)  128 us
    ppermute x10, starting transfers between devices, passed_along(): lax.ppermute(value, axis, [(source, source + steps) for source in range(f...  29.4 us
    dot_general x10, matrix products, outer_sum(): lax.dot_general(first_op, second_op, (((0,), (0,)), ((), ())), preferred_...  23.1 us
    unnamed x398, local copies, waits for them, and re-layouts  18.1 us
    dot_general x8, matrix products, back_dot(): lax.dot_general(first_op, second_op, (((1,), (1,)), ((), ())), preferred_...  17.1 us
  transfers between devices with their start and end apart: 18, of which 10 were waited for; matrix products, arithmetic and copies ran while one was open for 15% of the time, Pallas kernels for 0%

profile of v2, /device:TPU:0, one launch (start us, length us, event | category | flops | bytes accessed | tf_op | source)
XLA Modules:
  0.0 584.1 jit_solution(5257698811150695724)
XLA Ops:
  20.5 4.9 collective-permute-start.3
  25.4 3.5 collective-permute-start.2
  31.0 6.8 %all-gather.13.cloned.1.call-done = bf16[640,1548]{1,0:T(8,128)(2,1)} async-done(((bf16[160,1548]{1,0:T(8,128)(2,1)}), bf16[640,1548]{1,0:T(8,128)(2,1)}) %all-gather.13.cloned.1.call-update) | async-done | bytes 1981456 | tf_op jit(solution)/shard_map/all_gather | solution.py:512
  44.7 4.1 collective-permute-start.1
  48.8 3.7 collective-permute-start
  66.5 34.2 %all-gather.15.cloned.1.call-done = bf16[640,4096]{1,0:T(8,128)(2,1)} async-done(((bf16[160,4096]{1,0:T(8,128)(2,1)}), bf16[640,4096]{1,0:T(8,128)(2,1)}) %all-gather.15.cloned.1.call-update) | async-done | bytes 5242896 | tf_op jit(solution)/shard_map/all_gather | solution.py:512
  100.8 4.3 fusion.191
  108.7 19.6 %all-gather.23.cloned.1.call-done = bf16[1,2048,640]{2,1,0:T(8,128)(2,1)} async-done(((bf16[1,512,640]{2,1,0:T(8,128)(2,1)}), bf16[1,2048,640]{2,1,0:T(8,128)(2,1)}) %all-gather.23.cloned.1.call-update) | async-done | bytes 2621456 | tf_op jit(solution)/shard_map/all_gather | solution.py:512
  128.4 3.1 multiply_reduce_fusion.21
  132.7 19.0 %all-gather.17.cloned.1.call-done = bf16[640,1536]{1,0:T(8,128)(2,1)} async-done(((bf16[160,1536]{1,0:T(8,128)(2,1)}), bf16[640,1536]{1,0:T(8,128)(2,1)}) %all-gather.17.cloned.1.call-update) | async-done | bytes 1966096 | tf_op jit(solution)/shard_map/all_gather | solution.py:512
  156.3 4.1 collective-permute-start.5
  160.4 3.9 collective-permute-start.4
  179.9 2.4 multiply_reduce_fusion.19
  185.4 29.0 %all-gather.19.cloned.1.call-done = bf16[640,4096]{1,0:T(8,128)(2,1)} async-done(((bf16[160,4096]{1,0:T(8,128)(2,1)}), bf16[640,4096]{1,0:T(8,128)(2,1)}) %all-gather.19.cloned.1.call-update) | async-done | bytes 5242896 | tf_op jit(solution)/shard_map/all_gather | solution.py:512
  214.5 4.4 fusion.192
  222.5 19.7 %all-gather.27.cloned.1.call-done = bf16[1,2048,640]{2,1,0:T(8,128)(2,1)} async-done(((bf16[1,512,640]{2,1,0:T(8,128)(2,1)}), bf16[1,2048,640]{2,1,0:T(8,128)(2,1)}) %all-gather.27.cloned.1.call-update) | async-done | bytes 2621456 | tf_op jit(solution)/shard_map/all_gather | solution.py:512
  242.2 3.3 multiply_reduce_fusion.17
  248.5 2.5 fusion.31
  251.2 2.5 multiply_reduce_fusion.8
  259.7 3.7 fusion.187
  272.6 2.5 convolution_convert_fusion.3
  288.7 2.8 convolution_convert_fusion.9
  301.3 3.4 multiply_reduce_fusion.10
  307.0 2.5 fusion.24
  309.6 2.4 multiply_reduce_fusion.6
  314.8 3.6 fusion.189
  327.1 2.4 convolution_convert_fusion.1
  329.6 2.6 convolution_convert_fusion
  337.6 5.4 concatenate.152
  344.7 5.1 collective-permute-done.8
  360.2 3.6 concatenate.153
  363.8 198.4 %shard_map.272 = (bf16[160,2048]{1,0:T(8,128)(2,1)}, bf16[160,2048]{1,0:T(8,128)(2,1)}, bf16[512,640]{1,0:T(8,128)(2,1)}, bf16[160,2048]{1,0:T(8,128)(2,1)}, bf1...) custom-call(bf16[2,2,160,2048]{3,2,1,0:T(8,128)(2,1)} %bitcast.298, ...), custom_call_target="tpu_custom_call" | custom-call | tf_op jit(solution)/shard_map/pallas_call | solution.py:200
  (630 shorter events, 153.5 us)
Async XLA Ops:
  7.2 30.6 %all-gather.13.cloned.1.call-start = ((), (), s32[]{:S(2)}) async-start(), calls=%async_computation | async-start | bytes 2662400 | tf_op jit(solution)/shard_map/all_gather | solution.py:512
  12.2 51.4 %all-gather.21.cloned.1.call-start = ((), (), s32[]{:S(2)}) async-start(), calls=%async_computation.4 | async-start | bytes 1638400 | tf_op jit(solution)/shard_map/all_gather | solution.py:512
  13.1 87.6 %all-gather.15.cloned.1.call-start = ((), (), s32[]{:S(2)}) async-start(), calls=%async_computation.1 | async-start | bytes 6553600 | tf_op jit(solution)/shard_map/all_gather | solution.py:512
  15.9 112.5 %all-gather.23.cloned.1.call-start = ((), (), s32[]{:S(2)}) async-start(), calls=%async_computation.5 | async-start | bytes 3276800 | tf_op jit(solution)/shard_map/all_gather | solution.py:512
  17.7 134.0 %all-gather.17.cloned.1.call-start = ((), (), s32[]{:S(2)}) async-start(), calls=%async_computation.2 | async-start | bytes 2457600 | tf_op jit(solution)/shard_map/all_gather | solution.py:512
  18.6 161.3 %all-gather.25.cloned.1.call-start = ((), (), s32[]{:S(2)}) async-start(), calls=%async_computation.6 | async-start | bytes 1638400 | tf_op jit(solution)/shard_map/all_gather | solution.py:512
  19.2 195.3 %all-gather.19.cloned.1.call-start = ((), (), s32[]{:S(2)}) async-start(), calls=%async_computation.3 | async-start | bytes 6553600 | tf_op jit(solution)/shard_map/all_gather | solution.py:512
  20.4 221.8 %all-gather.27.cloned.1.call-start = ((), (), s32[]{:S(2)}) async-start(), calls=%async_computation.7 | async-start | bytes 3276800 | tf_op jit(solution)/shard_map/all_gather | solution.py:512
  20.5 9.1 %collective-permute-start.3 = (s32[256]{0:T(256)S(1)}, s32[256]{0:T(256)S(1)}, u32[]{:S(2)}, u32[]{:S(2)}) collective-permute-start(s32[256]{0:T(256)S(1)} %broadcast_add_fusion.2), channel_id=1, source_target_pairs={{0,4},{4,8},{8,12},{12,16},{16,20},{20,24},{24,28},{1,5},{5,9},{9,... | collective-permute-start | bytes 3080 | tf_op jit(solution)/shard_map/ppermute | solution.py:22
  25.4 4.8 collective-permute-start.2
  29.6 124.8 %copy-start.127 = (f32[1,256]{1,0:T(1,128)}, f32[1,256]{1,0:T(1,128)S(1)}, u32[]{:S(2)}) copy-start(f32[1,256]{1,0:T(1,128)S(1)} %convert_element_type.212) | copy-start | bytes 3076
  40.6 25.8 %copy-start.117 = (f32[640]{0:T(1024)}, f32[640]{0:T(1024)S(1)}, u32[]{:S(2)}) copy-start(f32[640]{0:T(1024)S(1)} %get-tuple-element.322) | copy-start | bytes 7684
  40.6 111.0 %copy-start.125 = (f32[640]{0:T(1024)}, f32[640]{0:T(1024)S(1)}, u32[]{:S(2)}) copy-start(f32[640]{0:T(1024)S(1)} %get-tuple-element.320) | copy-start | bytes 7684
  42.6 111.7 %copy-start.146 = (f32[1,256]{1,0:T(1,128)}, f32[1,256]{1,0:T(1,128)S(1)}, u32[]{:S(2)}) copy-start(f32[1,256]{1,0:T(1,128)S(1)} %get-tuple-element.395) | copy-start | bytes 3076
  43.9 14.6 %copy-start.71 = (bf16[256,128]{1,0:T(8,128)(2,1)}, bf16[256,128]{1,0:T(8,128)(2,1)S(1)}, u32[]{:S(2)}) copy-start(bf16[256,128]{1,0:T(8,128)(2,1)S(1)} %get-tuple-element.400) | copy-start | bytes 196612
  43.9 14.6 %copy-start.73 = (bf16[256,128]{1,0:T(8,128)(2,1)}, bf16[256,128]{1,0:T(8,128)(2,1)S(1)}, u32[]{:S(2)}) copy-start(bf16[256,128]{1,0:T(8,128)(2,1)S(1)} %get-tuple-element.401) | copy-start | bytes 196612
  44.7 10.4 %collective-permute-start.1 = (bf16[256,512]{1,0:T(8,128)(2,1)}, bf16[256,512]{1,0:T(8,128)(2,1)}, u32[]{:S(2)}, u32[]{:S(2)}) collective-permute-start(bf16[256,512]{1,0:T(8,128)(2,1)} %pad_maximum_fusion.18), channel_id=1, source_target_pairs={{0,4},{4,8},{8,12},{12,16},{16,20},{20,24},{24,28},{1,5},{5,9},{9,... | collective-permute-start | bytes 786440 | tf_op jit(solution)/shard_map/ppermute | solution.py:22
  48.8 8.7 %collective-permute-start = (bf16[256,512]{1,0:T(8,128)(2,1)}, bf16[256,512]{1,0:T(8,128)(2,1)}, u32[]{:S(2)}, u32[]{:S(2)}) collective-permute-start(bf16[256,512]{1,0:T(8,128)(2,1)} %pad_maximum_fusion.18), channel_id=1, source_target_pairs={{0,8},{4,12},{8,16},{12,20},{16,24},{20,28},{1,9},{5,13},{9,17},{1... | collective-permute-start | bytes 786440 | tf_op jit(solution)/shard_map/ppermute | solution.py:22
  65.8 39.3 %copy-start.136 = (f32[256]{0:T(256)}, f32[256]{0:T(256)S(1)}, u32[]{:S(2)}) copy-start(f32[256]{0:T(256)S(1)} %fusion.143) | copy-start | bytes 3076
  66.4 38.7 %copy-start.165 = (f32[256]{0:T(256)}, f32[256]{0:T(256)S(1)}, u32[]{:S(2)}) copy-start(f32[256]{0:T(256)S(1)} %get-tuple-element.332) | copy-start | bytes 3076
  66.4 38.7 %copy-start.156 = (f32[256]{0:T(256)}, f32[256]{0:T(256)S(1)}, u32[]{:S(2)}) copy-start(f32[256]{0:T(256)S(1)} %fusion.144) | copy-start | bytes 3076
  66.5 38.6 %copy-start.11 = (bf16[256,640]{1,0:T(8,128)(2,1)}, bf16[256,640]{1,0:T(8,128)(2,1)S(1)}, u32[]{:S(2)}) copy-start(bf16[256,640]{1,0:T(8,128)(2,1)S(1)} %multiply_convert_fusion.6) | copy-start | bytes 983044
  131.5 22.5 %copy-start.138 = (f32[256]{0:T(256)}, f32[256]{0:T(256)S(1)}, u32[]{:S(2)}) copy-start(f32[256]{0:T(256)S(1)} %fusion.145) | copy-start | bytes 3076
  132.6 21.4 %copy-start.8 = (f32[256,640]{1,0:T(8,128)}, f32[256,640]{1,0:T(8,128)S(1)}, u32[]{:S(2)}) copy-start(f32[256,640]{1,0:T(8,128)S(1)} %get-tuple-element.331) | copy-start | bytes 1966084
  132.6 21.4 %copy-start.167 = (f32[256]{0:T(256)}, f32[256]{0:T(256)S(1)}, u32[]{:S(2)}) copy-start(f32[256]{0:T(256)S(1)} %get-tuple-element.330) | copy-start | bytes 3076
  132.7 21.4 %copy-start.175 = (f32[256]{0:T(256)}, f32[256]{0:T(256)S(1)}, u32[]{:S(2)}) copy-start(f32[256]{0:T(256)S(1)} %fusion.146) | copy-start | bytes 3076
  156.3 15.1 %collective-permute-start.5 = (bf16[256,512]{1,0:T(8,128)(2,1)}, bf16[256,512]{1,0:T(8,128)(2,1)}, u32[]{:S(2)}, u32[]{:S(2)}) collective-permute-start(bf16[256,512]{1,0:T(8,128)(2,1)} %pad_maximum_fusion.19), channel_id=1, source_target_pairs={{0,4},{4,8},{8,12},{12,16},{16,20},{20,24},{24,28},{1,5},{5,9},{9,... | collective-permute-start | bytes 786440 | tf_op jit(solution)/shard_map/ppermute | solution.py:22
  160.4 12.2 %collective-permute-start.4 = (bf16[256,512]{1,0:T(8,128)(2,1)}, bf16[256,512]{1,0:T(8,128)(2,1)}, u32[]{:S(2)}, u32[]{:S(2)}) collective-permute-start(bf16[256,512]{1,0:T(8,128)(2,1)} %pad_maximum_fusion.19), channel_id=1, source_target_pairs={{0,8},{4,12},{8,16},{12,20},{16,24},{20,28},{1,9},{5,13},{9,17},{1... | collective-permute-start | bytes 786440 | tf_op jit(solution)/shard_map/ppermute | solution.py:22
  275.9 15.5 %collective-permute-start.7 = (bf16[256,512]{1,0:T(8,128)(2,1)}, bf16[256,512]{1,0:T(8,128)(2,1)}, u32[]{:S(2)}, u32[]{:S(2)}) collective-permute-start(bf16[256,512]{1,0:T(8,128)(2,1)} %pad_maximum_fusion.21), channel_id=1, source_target_pairs={{4,0},{8,4},{12,8},{16,12},{20,16},{24,20},{28,24},{5,1},{9,5},{13... | collective-permute-start | bytes 786440 | tf_op jit(solution)/shard_map/ppermute | solution.py:22
  277.9 15.2 %collective-permute-start.6 = (bf16[256,512]{1,0:T(8,128)(2,1)}, bf16[256,512]{1,0:T(8,128)(2,1)}, u32[]{:S(2)}, u32[]{:S(2)}) collective-permute-start(bf16[256,512]{1,0:T(8,128)(2,1)} %pad_maximum_fusion.20), channel_id=1, source_target_pairs={{8,0},{12,4},{16,8},{20,12},{24,16},{28,20},{9,1},{13,5},{17,9},{2... | collective-permute-start | bytes 786440 | tf_op jit(solution)/shard_map/ppermute | solution.py:22
  332.2 12.4 %collective-permute-start.9 = (bf16[256,512]{1,0:T(8,128)(2,1)S(1)}, bf16[256,512]{1,0:T(8,128)(2,1)S(1)}, u32[]{:S(2)}, u32[]{:S(2)}) collective-permute-start(bf16[256,512]{1,0:T(8,128)(2,1)S(1)} %pad_maximum_fusion.23), channel_id=1, source_target_pairs={{4,0},{8,4},{12,8},{16,12},{20,16},{24,20},{28,24},{5,1},{9,5},{13... | collective-permute-start | bytes 786440 | tf_op jit(solution)/shard_map/ppermute | solution.py:22
  333.6 16.2 %collective-permute-start.8 = (bf16[256,512]{1,0:T(8,128)(2,1)S(1)}, bf16[256,512]{1,0:T(8,128)(2,1)S(1)}, u32[]{:S(2)}, u32[]{:S(2)}) collective-permute-start(bf16[256,512]{1,0:T(8,128)(2,1)S(1)} %pad_maximum_fusion.22), channel_id=1, source_target_pairs={{8,0},{12,4},{16,8},{20,12},{24,16},{28,20},{9,1},{13,5},{17,9},{2... | collective-permute-start | bytes 786440 | tf_op jit(solution)/shard_map/ppermute | solution.py:22
  (185 other events, 642.1 us)
Sparse Core Ops, SparseCore 0:
  12.3 25.4 all-gather.12
  39.9 18.1 all-gather.20
  60.3 40.4 all-gather.14
  102.8 25.5 all-gather.22
  129.8 21.8 all-gather.16
  153.6 18.1 all-gather.24
  174.0 40.4 all-gather.18
  216.6 25.5 all-gather.26
